TPU v7x, 256 devices: a whole 4x4x8 slice. The times are simulated.
256 devices in a mesh: layer: 8 (over y, core), row: 32 (over z, x).
Axes of the slice: x: 4, y: 4, z: 8, core: 2. Of those that a mesh axis runs over, the one named last changes fastest.
Arguments:
- hidden_stack: bfloat16 [8, 3, 256, 28672], P('layer', None, 'row'), may hold values from -1.296875 to 1.296875
- model_stack: bfloat16 [8, 3, 256, 8192], P('layer', None, 'row'), may hold values from -1.296875 to 1.296875
- tenant_weights: float32 [8], replicated, may hold values from 0.5 to 2
- ranks: int32 [8], replicated, may hold values from 8 to 64, as said below
- start_basis: float32 [8, 256, 128], P('layer'), may hold values from -6 to 6
Outputs:
- serving_tiles: bfloat16 [8, 3, 2048, 8192], P(None, None, 'row', 'layer')
Inputs may be any that keep to these rules, and one draw needn't show every extreme that they name: The 8 ranks sum to 256; both the least and the most are taken by some tenant.
All inputs are finite; a program needn't handle non-finite values.
Results may differ from a plain program's by a relative error of at most 0.0057.
Values may be sent and summed in bfloat16 or wider, within the bound.
A program may use at most 128 MiB of HBM per device.

v0:
```python
import jax
import jax.numpy as jnp
from jax import lax
from jax.sharding import PartitionSpec as P

ITERS = 3
SERVE_DEV = 64
MOST_RANK = 64


def column_scale(ranks, tenant_weights, width):
    ends = jnp.cumsum(ranks)
    begins = ends - ranks
    columns = jnp.arange(width, dtype=jnp.int32)[:, None]
    owner = ((columns >= begins[None, :]) & (columns < ends[None, :])).astype(jnp.float32)
    factor = tenant_weights * jnp.sqrt(MOST_RANK / ranks.astype(jnp.float32))
    return jnp.dot(owner, factor, precision=lax.Precision.HIGHEST)


def cholesky_pass(matrix):
    product = jnp.dot(matrix.T, matrix, precision=lax.Precision.HIGHEST)
    factor = jnp.linalg.cholesky(product)
    return jax.scipy.linalg.solve_triangular(factor, matrix.T, lower=True).T


def orthonormal(matrix):
    return cholesky_pass(cholesky_pass(matrix))


def lower_solve(lower, basis):
    return jax.scipy.linalg.solve_triangular(lower, basis, lower=True, trans=1)


def shards(hidden_stack, model_stack, tenant_weights, ranks, start_basis):
    groups = lax.axis_size("row")
    layers = lax.axis_size("layer")
    width = hidden_stack.shape[2] * groups
    scale = column_scale(ranks, tenant_weights, width)
    outer = scale[:, None] * scale[None, :]
    model_local = model_stack[0]
    model_cols = model_local.shape[2]
    hidden_rows = lax.all_to_all(hidden_stack[0], "row", split_axis=2, concat_axis=1, tiled=True)
    model_rows = lax.all_to_all(model_local, "row", split_axis=2, concat_axis=1, tiled=True)
    gram_hidden = jnp.einsum(
        "prc,pqc->prq", hidden_rows, hidden_rows, preferred_element_type=jnp.float32
    )
    gram_model = jnp.einsum(
        "prc,pqc->prq", model_rows, model_rows, preferred_element_type=jnp.float32
    )
    moved = (hidden_rows, model_rows, gram_hidden, gram_model)
    hidden_rows = moved[0]
    model_rows = moved[1]
    gram_hidden, gram_model = lax.psum((moved[2], moved[3]), "row")
    lower = jnp.linalg.cholesky(gram_model * outer[None])
    basis = jnp.broadcast_to(start_basis[0], (3,) + start_basis.shape[1:])
    for sweep in range(ITERS):
        lifted = jnp.einsum("prq,pqk->prk", lower, basis, precision=lax.Precision.HIGHEST)
        pushed = jnp.einsum("prq,pqk->prk", gram_hidden, lifted, precision=lax.Precision.HIGHEST)
        raised = jnp.einsum("pqr,pqk->prk", lower, pushed, precision=lax.Precision.HIGHEST)
        basis = jax.vmap(orthonormal)(raised)
    lifted = jnp.einsum("prq,pqk->prk", lower, basis, precision=lax.Precision.HIGHEST)
    pulled = scale[None, :, None] * jax.vmap(lower_solve)(lower, basis)
    window = hidden_rows[:, :, :SERVE_DEV].astype(jnp.float32)
    left = jnp.einsum("prs,prk->psk", window, lifted, precision=lax.Precision.HIGHEST).astype(
        jnp.bfloat16
    )
    right = jnp.einsum(
        "prd,prk->pdk", model_rows.astype(jnp.float32), pulled, precision=lax.Precision.HIGHEST
    ).astype(jnp.bfloat16)
    block = model_cols // layers
    keep_width = right.shape[2]
    right_all = lax.all_gather(right, "row", axis=1, tiled=True)
    left_all = lax.all_gather(left[None], "layer", axis=0, tiled=True)
    blocks = right_all.reshape(3, layers, block, keep_width)
    blocks = lax.all_to_all(blocks, "layer", split_axis=1, concat_axis=1, tiled=True)
    tiles = jnp.einsum(
        "lpsk,pldk->lpsd", left_all, blocks, preferred_element_type=jnp.float32
    ).astype(jnp.bfloat16)
    return tiles


def solution(mesh):
    in_specs = (
        P("layer", None, "row", None),
        P("layer", None, "row", None),
        P(),
        P(),
        P("layer", None, None),
    )
    out_specs = P(None, None, "row", "layer")
    return jax.shard_map(shards, mesh=mesh, in_specs=in_specs, out_specs=out_specs, check_vma=False)
```

profile of v0, /device:TPU:8, one launch (start us, length us, event | category | flops | bytes accessed | tf_op | source)
XLA Modules:
  0.0 1189.5 jit_solution(5252003434759508400)
XLA Ops:
  6.5 9.5 copy.66
  24.1 13.6 %reshape.117 = bf16[32,2,3072]{2,1,0:T(2,128)(2,1)} reshape(bf16[8192,3,8]{2,1,0:T(4,128)(2,1)} %bitcast_bitcast_fusion.1) | data formatting | bytes 786432
  37.7 11.3 all-to-all-start
  49.0 26.8 %copy.72 = bf16[1,3,8,28672]{2,1,3,0:T(4,128)(2,1)} copy(bf16[1,3,8,28672]{3,2,1,0:T(8,128)(2,1)S(1)} %copy-done.6) | data formatting | bytes 2752512 | tf_op args[0]
  75.8 20.0 %bitcast_bitcast_fusion = bf16[28672,3,8]{2,1,0:T(4,128)(2,1)} fusion(bf16[1,3,8,28672]{2,1,3,0:T(4,128)(2,1)} %copy.72), kind=kLoop, calls=%fused_computation.114 | loop fusion | bytes 2752512
  95.8 34.1 %reshape.115 = bf16[32,2,10752]{2,1,0:T(2,128)(2,1)} reshape(bf16[28672,3,8]{2,1,0:T(4,128)(2,1)} %bitcast_bitcast_fusion) | data formatting | bytes 2752512
  129.9 9.8 all-to-all-start.1
  139.7 10.8 reshape.118
  150.5 9.8 copy.67
  161.5 12.6 %all-to-all-done.1 = bf16[32,2,10752]{2,1,0:T(2,128)(2,1)S(1)} async-done(((bf16[32,2,10752]{2,1,0:T(2,128)(2,1)}), bf16[32,2,10752]{2,1,0:T(2,128)(2,1)S(1)}, u32[]{:S(2)}, u32[]{:S(2)}) %all-to-all-start.1) | async-done | bytes 1376288 | tf_op jit(solution)/shard_map/all_to_all | solution.py:42
  174.1 29.1 %reshape.116 = bf16[28672,3,8]{2,1,0:T(4,128)(2,1)} reshape(bf16[32,2,10752]{2,1,0:T(2,128)(2,1)S(1)} %all-to-all-done.1) | data formatting | bytes 2752512
  203.2 33.9 %copy.73 = bf16[3,8,32,896]{3,1,2,0:T(8,128)(2,1)S(1)} copy(bf16[3,8,32,896]{1,0,3,2:T(4,128)(2,1)} %bitcast.174) | data formatting | bytes 2752512 | tf_op jit(solution)/shard_map/all_to_all | solution.py:42
  239.5 148.2 %all-reduce.4.cloned.1.call-done = (f32[3,256,256]{2,1,0:T(8,128)}, f32[3,256,256]{1,2,0:T(8,128)}) async-done(((f32[3,256,256]{2,1,0:T(8,128)}, f32[3,256,256]{1,2,0:T(8,128)}), (f32[3,256,256]{2,1,0:T(8,128)}, f32[3,256,256]{1,2,0:T(8,128)})) %all-reduce.4.cloned.1.call-update) | async-done | bytes 1572880 | tf_op jit(solution)/shard_map/psum | solution.py:53
  390.6 35.2 %custom-call.23 = f32[3,128,128]{2,1,0:T(8,128)S(1)} custom-call(f32[3,128,128]{2,1,0:T(8,128)S(1)} %cholesky.291), custom_call_target="Cholesky" | custom-call | tf_op jit(solution)/shard_map/jit(cholesky)/cholesky | solution.py:54
  425.9 29.5 %custom-call.24 = f32[3,1,128,128]{2,3,1,0:T(8,128)S(1)} custom-call(f32[3,1,128,128]{3,2,1,0:T(8,128)S(1)} %select_bitcast_fusion.6), custom_call_target="InvertDiagBlocksLowerTriangular" | custom-call | tf_op jit(solution)/shard_map/jit(cholesky)/cholesky | solution.py:54
  456.3 35.4 %custom-call.25 = f32[3,128,128]{2,1,0:T(8,128)S(1)} custom-call(f32[3,128,128]{2,1,0:T(8,128)S(1)} %convolution_subtract_fusion.1), custom_call_target="Cholesky" | custom-call | tf_op jit(solution)/shard_map/jit(cholesky)/cholesky | solution.py:54
  497.0 36.0 %custom-call.37 = f32[3,128,128]{2,1,0:T(8,128)S(1)} custom-call(f32[3,128,128]{2,1,0:T(8,128)} %fusion.35), custom_call_target="Cholesky" | custom-call | tf_op jit(solution)/shard_map/vmap(jit(cholesky))/cholesky | solution.py:22
  533.2 30.1 %custom-call.38 = f32[3,1,128,128]{2,3,1,0:T(8,128)} custom-call(f32[3,1,128,128]{3,2,1,0:T(8,128)S(1)} %select_bitcast_fusion.5), custom_call_target="InvertDiagBlocksLowerTriangular" | custom-call | tf_op jit(solution)/shard_map/vmap(jit(_solve_triangular))/triangular_solve | solution.py:23
  566.1 36.4 %custom-call.39 = f32[3,128,128]{2,1,0:T(8,128)S(1)} custom-call(f32[3,128,128]{2,1,0:T(8,128)} %fusion.33), custom_call_target="Cholesky" | custom-call | tf_op jit(solution)/shard_map/vmap(jit(cholesky))/cholesky | solution.py:22
  602.7 30.1 %custom-call.40 = f32[3,1,128,128]{2,3,1,0:T(8,128)} custom-call(f32[3,1,128,128]{3,2,1,0:T(8,128)S(1)} %select_bitcast_fusion.4), custom_call_target="InvertDiagBlocksLowerTriangular" | custom-call | tf_op jit(solution)/shard_map/vmap(jit(_solve_triangular))/triangular_solve | solution.py:23
  639.2 36.1 %custom-call.41 = f32[3,128,128]{2,1,0:T(8,128)S(1)} custom-call(f32[3,128,128]{2,1,0:T(8,128)} %fusion.30), custom_call_target="Cholesky" | custom-call | tf_op jit(solution)/shard_map/vmap(jit(cholesky))/cholesky | solution.py:22
  675.6 30.1 %custom-call.42 = f32[3,1,128,128]{2,3,1,0:T(8,128)} custom-call(f32[3,1,128,128]{3,2,1,0:T(8,128)S(1)} %select_bitcast_fusion.3), custom_call_target="InvertDiagBlocksLowerTriangular" | custom-call | tf_op jit(solution)/shard_map/vmap(jit(_solve_triangular))/triangular_solve | solution.py:23
  708.5 36.0 %custom-call.43 = f32[3,128,128]{2,1,0:T(8,128)S(1)} custom-call(f32[3,128,128]{2,1,0:T(8,128)} %fusion.28), custom_call_target="Cholesky" | custom-call | tf_op jit(solution)/shard_map/vmap(jit(cholesky))/cholesky | solution.py:22
  744.8 30.3 %custom-call.44 = f32[3,1,128,128]{2,3,1,0:T(8,128)} custom-call(f32[3,1,128,128]{3,2,1,0:T(8,128)S(1)} %select_bitcast_fusion.2), custom_call_target="InvertDiagBlocksLowerTriangular" | custom-call | tf_op jit(solution)/shard_map/vmap(jit(_solve_triangular))/triangular_solve | solution.py:23
  780.8 35.2 %custom-call.45 = f32[3,128,128]{2,1,0:T(8,128)S(1)} custom-call(f32[3,128,128]{2,1,0:T(8,128)S(1)} %fusion.25), custom_call_target="Cholesky" | custom-call | tf_op jit(solution)/shard_map/vmap(jit(cholesky))/cholesky | solution.py:22
  816.3 29.9 %custom-call.46 = f32[3,1,128,128]{2,3,1,0:T(8,128)S(1)} custom-call(f32[3,1,128,128]{3,2,1,0:T(8,128)S(1)} %select_bitcast_fusion.1), custom_call_target="InvertDiagBlocksLowerTriangular" | custom-call | tf_op jit(solution)/shard_map/vmap(jit(_solve_triangular))/triangular_solve | solution.py:23
  847.4 35.2 %custom-call.47 = f32[3,128,128]{2,1,0:T(8,128)S(1)} custom-call(f32[3,128,128]{2,1,0:T(8,128)S(1)} %fusion.23), custom_call_target="Cholesky" | custom-call | tf_op jit(solution)/shard_map/vmap(jit(cholesky))/cholesky | solution.py:22
  882.8 29.5 %custom-call.48 = f32[3,1,128,128]{2,3,1,0:T(8,128)S(1)} custom-call(f32[3,1,128,128]{3,2,1,0:T(8,128)S(1)} %select_bitcast_fusion), custom_call_target="InvertDiagBlocksLowerTriangular" | custom-call | tf_op jit(solution)/shard_map/vmap(jit(_solve_triangular))/triangular_solve | solution.py:23
  918.3 59.9 %custom-call.26 = f32[3,2,128,128]{2,3,1,0:T(8,128)S(1)} custom-call(f32[3,2,128,128]{3,2,1,0:T(8,128)} %bitcast.184), custom_call_target="InvertDiagBlocksLowerTriangular" | custom-call | tf_op jit(solution)/shard_map/vmap(jit(_solve_triangular))/triangular_solve | solution.py:31
  981.1 90.0 %all-gather.3.cloned.1.call-done = bf16[3,8192,128]{1,2,0:T(8,128)(2,1)} async-done(((bf16[3,256,128]{1,2,0:T(8,128)(2,1)}), bf16[3,8192,128]{1,2,0:T(8,128)(2,1)}) %all-gather.3.cloned.1.call-update) | async-done | bytes 6291472 | tf_op jit(solution)/shard_map/all_gather | solution.py:72
  1071.2 12.7 %copy.137 = bf16[48,8,8,1024]{3,2,1,0:T(8,128)(2,1)} copy(bf16[48,8,8,1024]{3,1,2,0:T(8,128)(2,1)} %bitcast.177) | data formatting | bytes 12582912
  1100.6 75.1 %all-gather = bf16[24,64,128]{2,1,0:T(8,128)(2,1)S(1)} all-gather(bf16[3,64,128]{2,1,0:T(8,128)(2,1)S(1)} %fusion.1), channel_id=2, replica_groups=mesh['layer'=8,'row'=32] {'layer'}, dimensions={0}, use_global_device_ids=true | all-gather | bytes 442368 | tf_op jit(solution)/shard_map/all_gather | solution.py:73
  (116 shorter events, 78.7 us)
Async XLA Ops:
  6.5 485.5 %copy-start = (f32[1,256,128]{2,1,0:T(8,128)S(1)}, f32[1,256,128]{2,1,0:T(8,128)}, u32[]{:S(2)}) copy-start(f32[1,256,128]{2,1,0:T(8,128)} %param.12) | copy-start | bytes 393220
  24.1 24.9 %copy-start.6 = (bf16[1,3,8,28672]{3,2,1,0:T(8,128)(2,1)S(1)}, bf16[1,3,8,28672]{3,2,1,0:T(8,128)(2,1)}, u32[]{:S(2)}) copy-start(bf16[1,3,8,28672]{3,2,1,0:T(8,128)(2,1)} %param.8) | copy-start | bytes 4128772
  37.7 92.2 %all-to-all-start = ((bf16[32,2,3072]{2,1,0:T(2,128)(2,1)}), bf16[32,2,3072]{2,1,0:T(2,128)(2,1)S(1)}, u32[]{:S(2)}, u32[]{:S(2)}) async-start(bf16[32,2,3072]{2,1,0:T(2,128)(2,1)} %reshape.117), calls=%async_computation | async-start | bytes 786432 | tf_op jit(solution)/shard_map/all_to_all | solution.py:43
  129.9 44.2 %all-to-all-start.1 = ((bf16[32,2,10752]{2,1,0:T(2,128)(2,1)}), bf16[32,2,10752]{2,1,0:T(2,128)(2,1)S(1)}, u32[]{:S(2)}, u32[]{:S(2)}) async-start(bf16[32,2,10752]{2,1,0:T(2,128)(2,1)} %reshape.115), calls=%async_computation.1 | async-start | bytes 2752512 | tf_op jit(solution)/shard_map/all_to_all | solution.py:42
  139.7 248.0 %all-reduce.4.cloned.1.call-start = ((), (), s32[]{:S(2)}) async-start(), calls=%async_computation.4 | async-start | bytes 3145728 | tf_op jit(solution)/shard_map/psum | solution.py:53
  160.3 42.9 %copy-start.2 = (bf16[3,8,32,256]{3,1,2,0:T(8,128)(2,1)}, bf16[3,8,32,256]{3,1,2,0:T(8,128)(2,1)S(1)}, u32[]{:S(2)}) copy-start(bf16[3,8,32,256]{3,1,2,0:T(8,128)(2,1)S(1)} %copy.67) | copy-start | bytes 1179652
  203.2 35.7 %copy-start.7 = (s32[8]{0:T(128)S(1)}, s32[8]{0:T(128)}, u32[]{:S(2)}) copy-start(s32[8]{0:T(128)} %param.11) | copy-start | bytes 100
  203.2 36.0 %copy-start.8 = (f32[8]{0:T(128)S(1)}, f32[8]{0:T(128)}, u32[]{:S(2)}) copy-start(f32[8]{0:T(128)} %param.10) | copy-start | bytes 100
  237.1 2.2 copy-start.5
  238.7 832.5 %all-gather.3.cloned.1.call-start = ((), (), s32[]{:S(2)}) async-start(), calls=%async_computation.3 | async-start | bytes 6488064 | tf_op jit(solution)/shard_map/all_gather | solution.py:72
  239.5 148.2 %copy-start.4 = (f32[256,256]{0,1:T(8,128)}, f32[256,256]{0,1:T(8,128)S(1)}, u32[]{:S(2)}) copy-start(f32[256,256]{0,1:T(8,128)S(1)} %broadcast_multiply_fusion.1) | copy-start | bytes 786436
  387.7 105.3 %copy-start.1 = (f32[3,256,256]{2,1,0:T(8,128)S(1)}, f32[3,256,256]{2,1,0:T(8,128)}, u32[]{:S(2)}) copy-start(f32[3,256,256]{2,1,0:T(8,128)} %get-tuple-element.25) | copy-start | bytes 2359300
  778.3 201.5 %copy-start.3 = (bf16[3,8,32,256]{3,1,2,0:T(8,128)(2,1)S(1)}, bf16[3,8,32,256]{3,1,2,0:T(8,128)(2,1)}, u32[]{:S(2)}) copy-start(bf16[3,8,32,256]{3,1,2,0:T(8,128)(2,1)} %copy-done.2) | copy-start | bytes 1179652
  1093.0 82.7 %all-to-all-start.2 = ((bf16[3,8,1024,128]{3,2,0,1:T(8,128)(2,1)}), bf16[3,8,1024,128]{3,2,0,1:T(8,128)(2,1)}, u32[]{:S(2)}, u32[]{:S(2)}) async-start(bf16[3,8,1024,128]{3,2,0,1:T(8,128)(2,1)} %copy.102), calls=%async_computation.2 | async-start | bytes 12582912 | tf_op jit(solution)/shard_map/all_to_all | solution.py:75
Sparse Core Ops, SparseCore 0:
  238.8 148.8 all-reduce.3
  981.2 89.8 all-gather.2
where the time goes:
time: 1200 us; the launch traced here: 1190 us
  other arithmetic  563 us (47%)
  waiting for transfers between devices  251 us (21%)
  local copies, waits for them, and re-layouts  224 us (19%)
  blocking collectives  75.1 us (6%)
  matrix products  36 us (3%)
  starting transfers between devices  26.7 us (2%)
  between operations  14.2 us (1%)
    another operation x18, other arithmetic, cholesky_pass(): factor = jnp.linalg.cholesky(product)  216 us
    another operation x12, other arithmetic, cholesky_pass(): return jax.scipy.linalg.solve_triangular(factor, matrix.T, lower=True).T  181 us
    unnamed x27, local copies, waits for them, and re-layouts  165 us
    psum x1, waiting for transfers between devices, shards(): gram_hidden, gram_model = lax.psum((moved[2], moved[3]), 'row')  148 us
    another operation x9, other arithmetic, shards(): lower = jnp.linalg.cholesky(gram_model * outer[None])  100 us
    all_gather x1, waiting for transfers between devices, shards(): right_all = lax.all_gather(right, 'row', axis=1, tiled=True)  90 us
    all_gather x1, blocking collectives, shards(): left_all = lax.all_gather(left[None], 'layer', axis=0, tiled=True)  75.1 us
    another operation x3, other arithmetic, lower_solve(): return jax.scipy.linalg.solve_triangular(lower, basis, lower=True, trans=1)  60.1 us
  transfers between devices with their start and end apart: 5, of which 3 were waited for; matrix products, arithmetic and copies ran while one was open for 9% of the time, Pallas kernels for 0%

commit v1 on v0

v1 whole, which is shorter than its diff:
```python
import functools
import jax
import jax.numpy as jnp
from jax import lax
from jax.experimental import pallas as pl
from jax.experimental.pallas import tpu as pltpu
from jax.sharding import PartitionSpec as P

ITERS = 3
SERVE_DEV = 64
MOST_RANK = 64
PROJ = 3
HI = lax.Precision.HIGHEST
MESH = pl.DeviceIdType.MESH
VM = pl.BlockSpec(memory_space=pltpu.VMEM)
ANY = pl.BlockSpec(memory_space=pl.ANY)
SM = pl.BlockSpec(memory_space=pltpu.SMEM)
VMEM_BYTES = 48 * 1024 * 1024


def dot_hi(a, b, dims):
    return lax.dot_general(a, b, (dims, ((), ())), precision=HI, preferred_element_type=jnp.float32)


def spread_lane(tile, lane):
    return jnp.broadcast_to(tile[:, lane:lane + 1], (8, 128))


def spread_row(tile, row):
    return jnp.broadcast_to(tile[row:row + 1, :], (8, 128))


def factor(matrix, need_upper, need_inverse):
    sub = lax.broadcasted_iota(jnp.int32, (8, 128), 0)
    lane = lax.broadcasted_iota(jnp.int32, (8, 128), 1)
    rows = [matrix[8 * k:8 * k + 8, :] for k in range(16)]
    inverse = [jnp.where(lane == sub + 8 * k, 1.0, 0.0).astype(jnp.float32) for k in range(16)]
    upper_rows, inverse_rows = [], []
    for k in range(16):
        panel, ipanel = rows[k], inverse[k]
        cols = [spread_lane(panel, 8 * k + c) for c in range(8)]
        raw, iraw, diag = panel, ipanel, panel
        for j in range(8):
            pivot = spread_row(cols[j], j)
            recip = 1.0 / pivot
            scaled = cols[j] * recip
            here = sub == j
            prow = spread_row(panel, j)
            irow = spread_row(ipanel, j)
            raw = jnp.where(here, prow, raw)
            iraw = jnp.where(here, irow, iraw)
            diag = jnp.where(here, pivot, diag)
            panel = jnp.where(here, prow * recip, panel - scaled * prow)
            if need_inverse:
                ipanel = jnp.where(here, irow * recip, ipanel - scaled * irow)
            for c in range(j + 1, 8):
                crow = spread_row(cols[c], j)
                cols[c] = jnp.where(here, crow * recip, cols[c] - scaled * crow)
        root = lax.rsqrt(diag)
        upper_rows.append(raw * root)
        inverse_rows.append(iraw * root)
        prows = [spread_row(panel, c) for c in range(8)]
        irows = [spread_row(ipanel, c) for c in range(8)]
        for i in range(k + 1, 16):
            coef = [spread_lane(rows[i], 8 * k + c) for c in range(8)]
            rows[i] = rows[i] - sum(coef[c] * prows[c] for c in range(8))
            if need_inverse:
                inverse[i] = inverse[i] - sum(coef[c] * irows[c] for c in range(8))
    out = []
    if need_upper:
        rowi = lax.broadcasted_iota(jnp.int32, (128, 128), 0)
        coli = lax.broadcasted_iota(jnp.int32, (128, 128), 1)
        up = jnp.concatenate(upper_rows, axis=0)
        out.append(jnp.where(coli >= rowi, up, 0.0))
    if need_inverse:
        out.append(jnp.concatenate(inverse_rows, axis=0))
    return out


def place():
    layer = lax.axis_index("layer")
    row = lax.axis_index("row")
    return layer, row, row // 4, row % 4


def remote(src, dst, send, recv, layer, row):
    return pltpu.make_async_remote_copy(
        src_ref=src, dst_ref=dst, send_sem=send, recv_sem=recv,
        device_id=(layer, row), device_id_type=MESH,
    )


def wait_bytes(ref, sem):
    pltpu.make_async_copy(ref, ref, sem).wait()


def pack_gram(buf, part):
    ranks = buf.shape[0] * buf.shape[1]
    factors = buf[...].astype(jnp.float32).reshape(ranks, buf.shape[2]).astype(jnp.bfloat16)
    gram = lax.dot_general(
        factors, factors, (((1,), (1,)), ((), ())), preferred_element_type=jnp.float32
    )
    part[:, :, 0:128] = gram[0:128, 0:128].reshape(8, 16, 128)
    part[:, :, 128:384] = gram[128:256, :].reshape(8, 16, 256)


def start_reduce(part, slots, send, recv, layer, z, x):
    def one(k, carry):
        to = (z + k) % 8
        remote(part.at[to], slots.at[z], send, recv, layer, to * 4 + x).start()
        return carry

    lax.fori_loop(1, 8, one, 0)
    slots[pl.ds(z, 1)] = part[pl.ds(z, 1)]


def start_share(slots, out, send, recv, send2, recv2, layer, z, x):
    wait_bytes(slots.at[pl.ds(0, 7)], recv)
    wait_bytes(slots.at[pl.ds(0, 7)], send)
    total = slots[0]
    for k in range(1, 8):
        total = total + slots[k]
    out[pl.ds(z, 1)] = total[None]

    def one(k, carry):
        to = (z + k) % 8
        remote(out.at[z], out.at[z], send2, recv2, layer, to * 4 + x).start()
        return carry

    lax.fori_loop(1, 8, one, 0)


def end_share(out, send2, recv2):
    wait_bytes(out.at[pl.ds(0, 7)], recv2)
    wait_bytes(out.at[pl.ds(0, 7)], send2)


def gram_kernel(f_ref, m_ref, gm_ref, gh_ref, mbuf, win, fbuf, part_m, part_h, slots_m, slots_h, sems):
    layer, row, z, x = place()
    barrier = pltpu.get_barrier_semaphore()

    def greet(k, carry):
        pl.semaphore_signal(barrier, inc=1, device_id=(layer, (row + k) % 32), device_id_type=MESH)
        return carry

    lax.fori_loop(1, 32, greet, 0)
    pl.semaphore_wait(barrier, 31)
    mwide, fwide = mbuf.shape[2], fbuf.shape[2]

    def pieces(src_ref, wide, to):
        column = pl.multiple_of((to // 4) * wide, 128)
        return src_ref.at[0, to % 4, :, pl.ds(column, wide)]

    for src_ref, buf, wide, base in ((m_ref, mbuf, mwide, 0), (f_ref, fbuf, fwide, 2)):
        def send(k, carry):
            to = (row + k) % 32

            @pl.when(to % 4 < PROJ)
            def _():
                remote(
                    pieces(src_ref, wide, to), buf.at[row], sems.at[base], sems.at[base + 1], layer, to
                ).start()

            return carry

        lax.fori_loop(1, 32, send, 0)

        @pl.when(x < PROJ)
        def _():
            pltpu.make_async_copy(pieces(src_ref, wide, row), buf.at[row], sems.at[base + 1]).start()

    @pl.when(x < PROJ)
    def _():
        wait_bytes(mbuf, sems.at[1])
        pack_gram(mbuf, part_m)
        start_reduce(part_m, slots_m, sems.at[4], sems.at[5], layer, z, x)
        start_share(slots_m, gm_ref, sems.at[4], sems.at[5], sems.at[6], sems.at[7], layer, z, x)
        wait_bytes(fbuf, sems.at[3])
        pack_gram(fbuf, part_h)
        start_reduce(part_h, slots_h, sems.at[8], sems.at[9], layer, z, x)
        for j in range(4):
            win[:, :, 128 * j:128 * j + 128] = fbuf[:, :, 896 * j:896 * j + 128]
        start_share(slots_h, gh_ref, sems.at[8], sems.at[9], sems.at[10], sems.at[11], layer, z, x)
        end_share(gm_ref, sems.at[6], sems.at[7])
        end_share(gh_ref, sems.at[10], sems.at[11])
        wait_bytes(mbuf.at[pl.ds(0, 23)], sems.at[0])
        wait_bytes(fbuf.at[pl.ds(0, 23)], sems.at[2])

    @pl.when(x >= PROJ)
    def _():
        wait_bytes(mbuf.at[pl.ds(0, 24)], sems.at[0])
        wait_bytes(fbuf.at[pl.ds(0, 24)], sems.at[2])


def column_scale(ranks_ref, weights_ref, index):
    total = jnp.zeros(index.shape, jnp.float32)
    begin = 0
    for t in range(8):
        end = begin + ranks_ref[t]
        rank = jnp.full(index.shape, ranks_ref[t].astype(jnp.float32))
        factor_t = weights_ref[t] * jnp.sqrt(MOST_RANK / rank)
        total = jnp.where((index >= begin) & (index < end), factor_t, total)
        begin = end
    return total


def core_kernel(gm_ref, gh_ref, mbuf, win, weights_ref, ranks_ref, start_ref, left_ref, right_ref,
                lower_s, upper_s, pulled_map, basis_s, both_s):
    row = lax.axis_index("row")

    @pl.when(row % 4 < PROJ)
    def _():
        scale_col = column_scale(ranks_ref, weights_ref, lax.broadcasted_iota(jnp.int32, (256, 1), 0))
        scale_row = column_scale(ranks_ref, weights_ref, lax.broadcasted_iota(jnp.int32, (1, 256), 1))
        packed = gm_ref[...].reshape(128, 384)
        first = packed[:, 0:128] * (scale_col[0:128] * scale_row[:, 0:128])
        cross = packed[:, 128:256] * (scale_col[128:256] * scale_row[:, 0:128])
        last = packed[:, 256:384] * (scale_col[128:256] * scale_row[:, 128:256])
        upper_first, inverse_first = factor(first, True, True)
        low = dot_hi(cross, inverse_first, ((1,), (1,)))
        (upper_last,) = factor(last - dot_hi(low, low, ((1,), (1,))), True, False)
        zero = jnp.zeros((128, 128), jnp.float32)
        upper_s[0:128, 0:128] = upper_first
        upper_s[0:128, 128:256] = low.T
        upper_s[128:256, 0:128] = zero
        upper_s[128:256, 128:256] = upper_last
        lower_s[0:128, 0:128] = upper_first.T
        lower_s[0:128, 128:256] = zero
        lower_s[128:256, 0:128] = low
        lower_s[128:256, 128:256] = upper_last.T
        packed = gh_ref[...].reshape(128, 384)
        hidden = jnp.concatenate(
            [
                jnp.concatenate([packed[:, 0:128], packed[:, 128:256].T], axis=1),
                packed[:, 128:384],
            ],
            axis=0,
        )
        pulled_map[...] = dot_hi(hidden, lower_s[...], ((1,), (0,)))
        basis_s[...] = start_ref[0]

        def sweep(_, carry):
            pushed = dot_hi(pulled_map[...], basis_s[...], ((1,), (0,)))
            both_s[0:256, :] = dot_hi(upper_s[...], pushed, ((1,), (0,)))
            both_s[256:512, :] = pushed

            def one_pass(_, inner):
                raised = both_s[0:256, :]
                (inverse,) = factor(dot_hi(raised, raised, ((0,), (0,))), False, True)
                both_s[...] = dot_hi(both_s[...], inverse, ((1,), (1,)))
                return inner

            lax.fori_loop(0, 2, one_pass, 0)
            basis_s[...] = both_s[0:256, :]
            return carry

        lax.fori_loop(0, ITERS, sweep, 0)
        lifted = dot_hi(lower_s[...], basis_s[...], ((1,), (0,)))
        pulled = scale_col * both_s[256:512, :]
        window = win[...].astype(jnp.float32).reshape(256, 512)
        left = dot_hi(window, lifted, ((0,), (0,)))
        for j in range(4):
            left_ref[j] = left[128 * j:128 * j + SERVE_DEV].astype(jnp.bfloat16)
        model = mbuf[...].astype(jnp.float32).reshape(256, 1024)
        right = dot_hi(pulled, model, ((0,), (0,))).astype(jnp.bfloat16)
        for c in range(8):
            right_ref[c] = right[:, 128 * c:128 * c + 128]


def gather_kernel(left_ref, right_ref, lall, rall, in_send, in_recv, left_send, left_recv,
                  ring_send, ring_recv, side_send, side_recv, wide_send, wide_recv, pass_send, pass_recv):
    layer, row, z, x = place()
    barrier = pltpu.get_barrier_semaphore()

    def greet(to_layer, to_row):
        pl.semaphore_signal(barrier, inc=1, device_id=(to_layer, to_row), device_id_type=MESH)

    def row_at(to_z, to_x):
        return (to_z % 8) * 4 + to_x % 4

    owner = layer == z
    real = x < PROJ
    for k in range(1, 8):
        greet((layer + k) % 8, row)
    for k in range(1, 4):
        greet(layer, row_at(z, x + k))
    greet(layer, row_at(z + 1, x))
    greet(layer, row_at(z + 7, x))
    @pl.when(real & (layer != z))
    def _():
        for l in range(8):
            ring_peer = (layer == (z + 1) % 8) | (layer == (z + 7) % 8)

            @pl.when(jnp.logical_not(ring_peer & (layer == l)))
            def _():
                greet(l, row_at(layer, x))

    pl.semaphore_wait(barrier, 12 + jnp.where(real, 7 - jnp.where(owner, 2, 0), 0))

    @pl.when(real)
    def _():
        for c in range(8):
            mine = rall.at[layer, x, c]

            @pl.when(owner & (z == c))
            def _():
                pltpu.make_async_copy(right_ref.at[c], mine, in_recv.at[0]).start()

            @pl.when(jnp.logical_not(owner & (z == c)))
            def _():
                remote(right_ref.at[c], mine, in_send.at[0], in_recv.at[0], z, row_at(c, x)).start()

        for k in range(1, 4):
            to = (x + k) % 4
            remote(left_ref.at[to], lall.at[layer, x], in_send.at[1], in_recv.at[1],
                   layer, row_at(z, to)).start()
        pltpu.make_async_copy(left_ref.at[x], lall.at[layer, x], in_recv.at[1]).start()

    wait_bytes(lall.at[layer], in_recv.at[1])
    for k in range(1, 8):
        to = (layer + k) % 8
        remote(lall.at[layer], lall.at[layer], left_send, left_recv, to, row).start()

    def shard(low, high, p, c):
        return rall.at[pl.ds(low, high - low), p, c % 8]

    def thick(low, high, c):
        return rall.at[pl.ds(low, high - low), :, c % 8]

    def ring(step, group):
        low = 4 * group
        cut = thick if group else lambda a, b, c: shard(a, b, x, c)
        up_high = low + (4 if step < 3 else 2)
        down_low = low + (0 if step < 3 else 2)
        up = remote(cut(low, up_high, z + 8 - step), cut(low, up_high, z + 8 - step),
                    ring_send.at[group, 0, step], ring_recv.at[group, 0, step], layer, row_at(z + 1, x))
        down = remote(cut(down_low, low + 4, z + step), cut(down_low, low + 4, z + step),
                      ring_send.at[group, 1, step], ring_recv.at[group, 1, step], layer, row_at(z + 7, x))
        return up, down

    def ring_got(step, group):
        low = 4 * group
        cut = thick if group else lambda a, b, c: shard(a, b, x, c)
        up_high = low + (4 if step < 3 else 2)
        down_low = low + (0 if step < 3 else 2)
        wait_bytes(cut(low, up_high, z + 7 - step), ring_recv.at[group, 0, step])
        wait_bytes(cut(down_low, low + 4, z + 1 + step), ring_recv.at[group, 1, step])

    def columns(turn):
        if turn == 0:
            return (z,)
        if turn == 4:
            return (z + 4,)
        return (z + 8 - turn, z + turn)

    def widen(turn):
        for n, c in enumerate(columns(turn)):
            piece = shard(0, 4, x, c)
            remote(piece, piece, wide_send.at[0, turn, n], wide_recv.at[0, turn, n],
                   layer, row_at(z, x + 1)).start()
            remote(piece, piece, wide_send.at[1, turn, n], wide_recv.at[1, turn, n],
                   layer, row_at(z, x + 3)).start()

    def widen_sent(turn):
        for n, c in enumerate(columns(turn)):
            piece = shard(0, 4, x, c)
            wait_bytes(piece, wide_send.at[0, turn, n])
            wait_bytes(piece, wide_send.at[1, turn, n])

    before, after = (x + 3) % 4, (x + 1) % 4

    def relay(turn):
        for n, c in enumerate(columns(turn)):
            @pl.when(before < PROJ)
            def _():
                wait_bytes(shard(0, 4, before, c), wide_recv.at[0, turn, n])
                piece = shard(0, 2, before, c)
                remote(piece, piece, pass_send.at[0, turn, n], pass_recv.at[0, turn, n],
                       layer, row_at(z, x + 1)).start()

            @pl.when(after < PROJ)
            def _():
                wait_bytes(shard(0, 4, after, c), wide_recv.at[1, turn, n])
                piece = shard(2, 4, after, c)
                remote(piece, piece, pass_send.at[1, turn, n], pass_recv.at[1, turn, n],
                       layer, row_at(z, x + 3)).start()

    def relay_end(turn):
        far = (x + 2) % 4
        for n, c in enumerate(columns(turn)):
            @pl.when(before < PROJ)
            def _():
                wait_bytes(shard(0, 2, before, c), pass_send.at[0, turn, n])

            @pl.when(after < PROJ)
            def _():
                wait_bytes(shard(2, 4, after, c), pass_send.at[1, turn, n])

            @pl.when(far < PROJ)
            def _():
                wait_bytes(shard(0, 2, far, c), pass_recv.at[0, turn, n])
                wait_bytes(shard(2, 4, far, c), pass_recv.at[1, turn, n])

    @pl.when(real)
    def _():
        wait_bytes(rall.at[:, x, z], in_recv.at[0])
        piece = shard(4, 8, x, z)
        for k in range(1, 4):
            remote(piece, piece, side_send.at[k - 1], side_recv.at[k - 1], layer, row_at(z, x + k)).start()
        for copy in ring(0, 0):
            copy.start()
        widen(0)

    for k in range(1, 4):
        source = (x + 4 - k) % 4

        @pl.when(source < PROJ)
        def _():
            wait_bytes(shard(4, 8, source, z), side_recv.at[k - 1])

    for copy in ring(0, 1):
        copy.start()
    for step in range(4):
        @pl.when(real)
        def _():
            ring_got(step, 0)
            if step < 3:
                for copy in ring(step + 1, 0):
                    copy.start()
            widen(step + 1)

        ring_got(step, 1)
        if step < 3:
            for copy in ring(step + 1, 1):
                copy.start()
        relay(step)
    relay(4)
    for turn in range(5):
        relay_end(turn)
    for step in range(4):
        for copy in ring(step, 1):
            copy.wait_send()

    @pl.when(real)
    def _():
        for turn in range(5):
            widen_sent(turn)
        for step in range(4):
            for copy in ring(step, 0):
                copy.wait_send()
        piece = shard(4, 8, x, z)
        for k in range(1, 4):
            wait_bytes(piece, side_send.at[k - 1])

        @pl.when(owner)
        def _():
            wait_bytes(right_ref.at[pl.ds(0, 7)], in_send.at[0])

        @pl.when(jnp.logical_not(owner))
        def _():
            wait_bytes(right_ref, in_send.at[0])

        wait_bytes(left_ref.at[pl.ds(0, 3)], in_send.at[1])

    wait_bytes(lall.at[pl.ds(0, 7)], left_send)
    wait_bytes(lall.at[pl.ds(0, 7)], left_recv)


def tile_kernel(left_ref, right_ref, out_ref):
    right = jnp.concatenate([right_ref[0, 0, c] for c in range(8)], axis=1)
    out_ref[0, 0] = jnp.dot(
        left_ref[0, 0], right, preferred_element_type=jnp.float32
    ).astype(jnp.bfloat16)


def shards(hidden_stack, model_stack, tenant_weights, ranks, start_basis):
    f32, bf16 = jnp.float32, jnp.bfloat16
    shape = jax.ShapeDtypeStruct
    sem = pltpu.SemaphoreType.DMA
    gm, gh, mbuf, win = pl.pallas_call(
        gram_kernel,
        out_shape=[
            shape((8, 16, 384), f32), shape((8, 16, 384), f32),
            shape((32, 8, 1024), bf16), shape((32, 8, 512), bf16),
        ],
        in_specs=[ANY, ANY],
        out_specs=[VM] * 4,
        scratch_shapes=[
            pltpu.VMEM((32, 8, 3584), bf16),
            pltpu.VMEM((8, 16, 384), f32), pltpu.VMEM((8, 16, 384), f32),
            pltpu.VMEM((8, 16, 384), f32), pltpu.VMEM((8, 16, 384), f32),
            sem((12,)),
        ],
        compiler_params=pltpu.CompilerParams(
            collective_id=0, has_side_effects=True, vmem_limit_bytes=VMEM_BYTES
        ),
    )(hidden_stack, model_stack)
    left, right = pl.pallas_call(
        core_kernel,
        out_shape=[shape((4, SERVE_DEV, 128), bf16), shape((8, 128, 128), bf16)],
        in_specs=[VM, VM, VM, VM, SM, SM, VM],
        out_specs=[VM, VM],
        scratch_shapes=[
            pltpu.VMEM((256, 256), f32), pltpu.VMEM((256, 256), f32), pltpu.VMEM((256, 256), f32),
            pltpu.VMEM((256, 128), f32), pltpu.VMEM((512, 128), f32),
        ],
        compiler_params=pltpu.CompilerParams(vmem_limit_bytes=VMEM_BYTES),
    )(gm, gh, mbuf, win, tenant_weights, ranks, start_basis)
    lall, rall = pl.pallas_call(
        gather_kernel,
        out_shape=[shape((8, PROJ, SERVE_DEV, 128), bf16), shape((8, PROJ, 8, 128, 128), bf16)],
        in_specs=[ANY, ANY],
        out_specs=[ANY, ANY],
        scratch_shapes=[
            sem((2,)), sem((2,)), sem, sem,
            sem((2, 2, 4)), sem((2, 2, 4)), sem((3,)), sem((3,)),
            sem((2, 5, 2)), sem((2, 5, 2)), sem((2, 5, 2)), sem((2, 5, 2)),
        ],
        compiler_params=pltpu.CompilerParams(collective_id=1, has_side_effects=True),
    )(left, right)
    return pl.pallas_call(
        tile_kernel,
        grid=(8, PROJ),
        out_shape=shape((8, PROJ, SERVE_DEV, 1024), bf16),
        in_specs=[
            pl.BlockSpec((1, 1, SERVE_DEV, 128), lambda l, p: (l, p, 0, 0)),
            pl.BlockSpec((1, 1, 8, 128, 128), lambda l, p: (l, p, 0, 0, 0)),
        ],
        out_specs=pl.BlockSpec((1, 1, SERVE_DEV, 1024), lambda l, p: (l, p, 0, 0)),
    )(lall, rall)


def solution(mesh):
    in_specs = (
        P("layer", None, "row", None),
        P("layer", None, "row", None),
        P(),
        P(),
        P("layer", None, None),
    )
    out_specs = P(None, None, "row", "layer")
    return jax.shard_map(shards, mesh=mesh, in_specs=in_specs, out_specs=out_specs, check_vma=False)
```

time: 1200 us -> 209 us (0.17)
  other arithmetic: 563 us -> 0 us
  waiting for transfers between devices: 251 us -> 0 us
  local copies, waits for them, and re-layouts: 224 us -> 5.86 us
  Pallas kernels: 0 us -> 202 us
  blocking collectives: 75.1 us -> 0 us
  matrix products: 36 us -> 0 us
  starting transfers between devices: 26.7 us -> 0 us
  between operations: 14.2 us -> 0.05 us
    another operation x43 -> x0, other arithmetic: 557 us -> none  [the longest x18 216 us: cholesky_pass(): factor = jnp.linalg.cholesky(product)]
    pallas_call x0 -> x4, Pallas kernels: none -> 202 us  [the longest x1 70.6 us: shards(): pl.pallas_call(gram_kernel, out_shape=[shape((8, 16, 384), f32), shape((8...]
    unnamed x27 -> x14, local copies, waits for them, and re-layouts: 165 us -> 5.86 us
    psum x1 -> x0, waiting for transfers between devices: 148 us -> none  [shards(): gram_hidden, gram_model = lax.psum((moved[2], moved[3]), 'row')]
    all_gather x1 -> x0, waiting for transfers between devices: 90 us -> none  [shards(): right_all = lax.all_gather(right, 'row', axis=1, tiled=True)]
    all_gather x1 -> x0, blocking collectives: 75.1 us -> none  [shards(): left_all = lax.all_gather(left[None], 'layer', axis=0, tiled=True)]
    all_to_all x2 -> x0, local copies, waits for them, and re-layouts: 43.7 us -> none  [the longest x1 33.9 us: shards(): lax.all_to_all(hidden_stack[0], 'row', split_axis=2, concat_axis=1, tiled...]
    dot_general x22 -> x0, matrix products: 26.8 us -> none  [the longest x1 6.74 us: shards(): jnp.einsum('lpsk,pldk->lpsd', left_all, blocks, preferred_element_type=jn...]
  transfers between devices with their start and end apart: 5 -> 0, of which waited for: 3 -> 0; matrix products, arithmetic and copies ran while one was open for 9% -> 0% of each run, Pallas kernels for 0% -> 0%
where the time goes in v1:
time: 209 us; the launch traced here: 208 us
  Pallas kernels  202 us (97%)
  local copies, waits for them, and re-layouts  5.86 us (3%)
    pallas_call x1, Pallas kernels, shards(): pl.pallas_call(gram_kernel, out_shape=[shape((8, 16, 384), f32), shape((8...  70.6 us
    pallas_call x1, Pallas kernels, shards(): pl.pallas_call(gather_kernel, out_shape=[shape((8, PROJ, SERVE_DEV, 128),...  67 us
    pallas_call x1, Pallas kernels, shards(): pl.pallas_call(core_kernel, out_shape=[shape((4, SERVE_DEV, 128), bf16),...  48.6 us
    pallas_call x1, Pallas kernels, shards(): pl.pallas_call(tile_kernel, grid=(8, PROJ), out_shape=shape((8, PROJ, SER...  15.9 us
    unnamed x14, local copies, waits for them, and re-layouts  5.86 us

profile of v1, /device:TPU:8, one launch (start us, length us, event | category | flops | bytes accessed | tf_op | source)
XLA Modules:
  0.0 208.0 jit_solution(1138918136088133562)
XLA Ops:
  0.0 0.0 copy-start
  0.0 1.3 copy-done
  1.3 0.0 copy-start.1
  1.3 1.0 copy-done.1
  2.3 70.6 %shard_map.55 = (f32[8,16,384]{2,1,0:T(8,128)S(1)}, f32[8,16,384]{2,1,0:T(8,128)S(1)}, bf16[32,8,1024]{2,1,0:T(8,128)(2,1)S(1)}, bf16[32,8,512]{2,1,0:T(8,128)(2,1)S(1)}) custom-call(bf16[1,3,8,28672]{3,2,1,0:T(8,128)(2,1)S(1)} %copy-done, bf16[1,3,8,8192]{3,2,1,0:T(8,128)(2,1)S(1)} %copy-done.1), custom_call_target="tpu_custom_call" | custom-call | tf_op jit(solution)/shard_map/pallas_call | solution.py:480
  72.9 0.0 copy-start.3
  72.9 0.9 copy-done.3
  73.8 0.0 copy-start.5
  73.8 0.7 copy-done.5
  74.5 0.0 copy-start.6
  74.5 0.7 copy-done.6
  75.1 48.6 %shard_map.56 = (bf16[4,64,128]{2,1,0:T(8,128)(2,1)S(1)}, bf16[8,128,128]{2,1,0:T(8,128)(2,1)S(1)}) custom-call(f32[8,16,384]{2,1,0:T(8,128)S(1)} %get-tuple-element.13.gm_ref, f32[8,16,384]{2,1,0:T(8,128)S(1)} %get-tuple-element.14.gh_ref, bf16[32,8,1024]{2,1,0:T(8,128)(2,1)S(1)} %get-tuple-element.15.mbuf, bf16[32,8,512]{2,1,0:T(8,128)(2,1)S(1)} %get-tuple-element.16.win, ...), custom_call_target="tpu_custom_call" | custom-call | tf_op jit(solution)/shard_map/pallas_call | solution.py:498
  123.8 0.0 copy-start.2
  123.8 0.7 copy-done.2
  124.5 0.0 copy-start.4
  124.5 0.6 copy-done.4
  125.1 67.0 %shard_map.57 = (bf16[8,3,64,128]{3,2,1,0:T(8,128)(2,1)}, bf16[8,3,8,128,128]{4,3,2,1,0:T(8,128)(2,1)}) custom-call(bf16[4,64,128]{2,1,0:T(8,128)(2,1)} %copy-done.4, bf16[8,128,128]{2,1,0:T(8,128)(2,1)} %copy-done.2), custom_call_target="tpu_custom_call" | custom-call | tf_op jit(solution)/shard_map/pallas_call | solution.py:509
  192.1 15.9 %shard_map.58 = bf16[8,3,64,1024]{3,2,1,0:T(8,128)(2,1)} custom-call(bf16[8,3,64,128]{3,2,1,0:T(8,128)(2,1)} %get-tuple-element.19.left_ref, bf16[8,3,8,128,128]{4,3,2,1,0:T(8,128)(2,1)} %get-tuple-element.20.right_ref), custom_call_target="tpu_custom_call" | custom-call | tf_op jit(solution)/shard_map/pallas_call | solution.py:521
Async XLA Ops:
  0.0 1.3 copy-start
  1.3 1.0 copy-start.1
  72.9 0.9 copy-start.3
  73.8 0.7 copy-start.5
  74.5 0.7 copy-start.6
  123.8 0.7 copy-start.2
  124.5 0.6 copy-start.4

commit v2 on v1

--- a/solution.py
+++ b/solution.py
@@ -135,7 +135,9 @@
     wait_bytes(out.at[pl.ds(0, 7)], send2)
 
 
-def gram_kernel(f_ref, m_ref, gm_ref, gh_ref, mbuf, win, fbuf, part_m, part_h, slots_m, slots_h, sems):
+def core_kernel(f_ref, m_ref, weights_ref, ranks_ref, start_ref, left_ref, right_ref, mbuf, fbuf,
+                part_m, part_h, slots_m, slots_h, gm_ref, gh_ref,
+                lower_s, upper_s, pulled_map, basis_s, both_s, sems):
     layer, row, z, x = place()
     barrier = pltpu.get_barrier_semaphore()
 
@@ -175,14 +177,15 @@
         pack_gram(mbuf, part_m)
         start_reduce(part_m, slots_m, sems.at[4], sems.at[5], layer, z, x)
         start_share(slots_m, gm_ref, sems.at[4], sems.at[5], sems.at[6], sems.at[7], layer, z, x)
+        end_share(gm_ref, sems.at[6], sems.at[7])
+        lower_factor(gm_ref, weights_ref, ranks_ref, lower_s, upper_s)
         wait_bytes(fbuf, sems.at[3])
         pack_gram(fbuf, part_h)
         start_reduce(part_h, slots_h, sems.at[8], sems.at[9], layer, z, x)
-        for j in range(4):
-            win[:, :, 128 * j:128 * j + 128] = fbuf[:, :, 896 * j:896 * j + 128]
         start_share(slots_h, gh_ref, sems.at[8], sems.at[9], sems.at[10], sems.at[11], layer, z, x)
-        end_share(gm_ref, sems.at[6], sems.at[7])
         end_share(gh_ref, sems.at[10], sems.at[11])
+        iterate(gh_ref, start_ref, lower_s, upper_s, pulled_map, basis_s, both_s)
+        truncated(mbuf, fbuf, weights_ref, ranks_ref, lower_s, basis_s, both_s, left_ref, right_ref)
         wait_bytes(mbuf.at[pl.ds(0, 23)], sems.at[0])
         wait_bytes(fbuf.at[pl.ds(0, 23)], sems.at[2])
 
@@ -204,67 +207,69 @@
     return total
 
 
-def core_kernel(gm_ref, gh_ref, mbuf, win, weights_ref, ranks_ref, start_ref, left_ref, right_ref,
-                lower_s, upper_s, pulled_map, basis_s, both_s):
-    row = lax.axis_index("row")
-
-    @pl.when(row % 4 < PROJ)
-    def _():
-        scale_col = column_scale(ranks_ref, weights_ref, lax.broadcasted_iota(jnp.int32, (256, 1), 0))
-        scale_row = column_scale(ranks_ref, weights_ref, lax.broadcasted_iota(jnp.int32, (1, 256), 1))
-        packed = gm_ref[...].reshape(128, 384)
-        first = packed[:, 0:128] * (scale_col[0:128] * scale_row[:, 0:128])
-        cross = packed[:, 128:256] * (scale_col[128:256] * scale_row[:, 0:128])
-        last = packed[:, 256:384] * (scale_col[128:256] * scale_row[:, 128:256])
-        upper_first, inverse_first = factor(first, True, True)
-        low = dot_hi(cross, inverse_first, ((1,), (1,)))
-        (upper_last,) = factor(last - dot_hi(low, low, ((1,), (1,))), True, False)
-        zero = jnp.zeros((128, 128), jnp.float32)
-        upper_s[0:128, 0:128] = upper_first
-        upper_s[0:128, 128:256] = low.T
-        upper_s[128:256, 0:128] = zero
-        upper_s[128:256, 128:256] = upper_last
-        lower_s[0:128, 0:128] = upper_first.T
-        lower_s[0:128, 128:256] = zero
-        lower_s[128:256, 0:128] = low
-        lower_s[128:256, 128:256] = upper_last.T
-        packed = gh_ref[...].reshape(128, 384)
-        hidden = jnp.concatenate(
-            [
-                jnp.concatenate([packed[:, 0:128], packed[:, 128:256].T], axis=1),
-                packed[:, 128:384],
-            ],
-            axis=0,
-        )
-        pulled_map[...] = dot_hi(hidden, lower_s[...], ((1,), (0,)))
-        basis_s[...] = start_ref[0]
-
-        def sweep(_, carry):
-            pushed = dot_hi(pulled_map[...], basis_s[...], ((1,), (0,)))
-            both_s[0:256, :] = dot_hi(upper_s[...], pushed, ((1,), (0,)))
-            both_s[256:512, :] = pushed
-
-            def one_pass(_, inner):
-                raised = both_s[0:256, :]
-                (inverse,) = factor(dot_hi(raised, raised, ((0,), (0,))), False, True)
-                both_s[...] = dot_hi(both_s[...], inverse, ((1,), (1,)))
-                return inner
-
-            lax.fori_loop(0, 2, one_pass, 0)
-            basis_s[...] = both_s[0:256, :]
-            return carry
-
-        lax.fori_loop(0, ITERS, sweep, 0)
-        lifted = dot_hi(lower_s[...], basis_s[...], ((1,), (0,)))
-        pulled = scale_col * both_s[256:512, :]
-        window = win[...].astype(jnp.float32).reshape(256, 512)
+def lower_factor(gm_ref, weights_ref, ranks_ref, lower_s, upper_s):
+    scale_col = column_scale(ranks_ref, weights_ref, lax.broadcasted_iota(jnp.int32, (256, 1), 0))
+    scale_row = column_scale(ranks_ref, weights_ref, lax.broadcasted_iota(jnp.int32, (1, 256), 1))
+    packed = gm_ref[...].reshape(128, 384)
+    first = packed[:, 0:128] * (scale_col[0:128] * scale_row[:, 0:128])
+    cross = packed[:, 128:256] * (scale_col[128:256] * scale_row[:, 0:128])
+    last = packed[:, 256:384] * (scale_col[128:256] * scale_row[:, 128:256])
+    upper_first, inverse_first = factor(first, True, True)
+    low = dot_hi(cross, inverse_first, ((1,), (1,)))
+    (upper_last,) = factor(last - dot_hi(low, low, ((1,), (1,))), True, False)
+    zero = jnp.zeros((128, 128), jnp.float32)
+    upper_s[0:128, 0:128] = upper_first
+    upper_s[0:128, 128:256] = low.T
+    upper_s[128:256, 0:128] = zero
+    upper_s[128:256, 128:256] = upper_last
+    lower_s[0:128, 0:128] = upper_first.T
+    lower_s[0:128, 128:256] = zero
+    lower_s[128:256, 0:128] = low
+    lower_s[128:256, 128:256] = upper_last.T
+
+
+def iterate(gh_ref, start_ref, lower_s, upper_s, pulled_map, basis_s, both_s):
+    packed = gh_ref[...].reshape(128, 384)
+    hidden = jnp.concatenate(
+        [
+            jnp.concatenate([packed[:, 0:128], packed[:, 128:256].T], axis=1),
+            packed[:, 128:384],
+        ],
+        axis=0,
+    )
+    pulled_map[...] = dot_hi(hidden, lower_s[...], ((1,), (0,)))
+    basis_s[...] = start_ref[0]
+
+    def sweep(_, carry):
+        pushed = dot_hi(pulled_map[...], basis_s[...], ((1,), (0,)))
+        both_s[0:256, :] = dot_hi(upper_s[...], pushed, ((1,), (0,)))
+        both_s[256:512, :] = pushed
+
+        def one_pass(_, inner):
+            raised = both_s[0:256, :]
+            (inverse,) = factor(dot_hi(raised, raised, ((0,), (0,))), False, True)
+            both_s[...] = dot_hi(both_s[...], inverse, ((1,), (1,)))
+            return inner
+
+        lax.fori_loop(0, 2, one_pass, 0)
+        basis_s[...] = both_s[0:256, :]
+        return carry
+
+    lax.fori_loop(0, ITERS, sweep, 0)
+
+
+def truncated(mbuf, fbuf, weights_ref, ranks_ref, lower_s, basis_s, both_s, left_ref, right_ref):
+    scale_col = column_scale(ranks_ref, weights_ref, lax.broadcasted_iota(jnp.int32, (256, 1), 0))
+    lifted = dot_hi(lower_s[...], basis_s[...], ((1,), (0,)))
+    pulled = scale_col * both_s[256:512, :]
+    for j in range(4):
+        window = fbuf[:, :, 896 * j:896 * j + 128].astype(jnp.float32).reshape(256, 128)
         left = dot_hi(window, lifted, ((0,), (0,)))
-        for j in range(4):
-            left_ref[j] = left[128 * j:128 * j + SERVE_DEV].astype(jnp.bfloat16)
-        model = mbuf[...].astype(jnp.float32).reshape(256, 1024)
-        right = dot_hi(pulled, model, ((0,), (0,))).astype(jnp.bfloat16)
-        for c in range(8):
-            right_ref[c] = right[:, 128 * c:128 * c + 128]
+        left_ref[j] = left[0:SERVE_DEV].astype(jnp.bfloat16)
+    model = mbuf[...].astype(jnp.float32).reshape(256, 1024)
+    right = dot_hi(pulled, model, ((0,), (0,))).astype(jnp.bfloat16)
+    for c in range(8):
+        right_ref[c] = right[:, 128 * c:128 * c + 128]
 
 
 def gather_kernel(left_ref, right_ref, lall, rall, in_send, in_recv, left_send, left_recv,
@@ -467,45 +472,34 @@
 
 
 def tile_kernel(left_ref, right_ref, out_ref):
-    right = jnp.concatenate([right_ref[0, 0, c] for c in range(8)], axis=1)
-    out_ref[0, 0] = jnp.dot(
-        left_ref[0, 0], right, preferred_element_type=jnp.float32
-    ).astype(jnp.bfloat16)
+    for p in range(PROJ):
+        right = jnp.concatenate([right_ref[0, p, c] for c in range(8)], axis=1)
+        out_ref[0, p] = jnp.dot(
+            left_ref[0, p], right, preferred_element_type=jnp.float32
+        ).astype(jnp.bfloat16)
 
 
 def shards(hidden_stack, model_stack, tenant_weights, ranks, start_basis):
     f32, bf16 = jnp.float32, jnp.bfloat16
     shape = jax.ShapeDtypeStruct
     sem = pltpu.SemaphoreType.DMA
-    gm, gh, mbuf, win = pl.pallas_call(
-        gram_kernel,
-        out_shape=[
-            shape((8, 16, 384), f32), shape((8, 16, 384), f32),
-            shape((32, 8, 1024), bf16), shape((32, 8, 512), bf16),
-        ],
-        in_specs=[ANY, ANY],
-        out_specs=[VM] * 4,
+    gram = pltpu.VMEM((8, 16, 384), f32)
+    left, right = pl.pallas_call(
+        core_kernel,
+        out_shape=[shape((4, SERVE_DEV, 128), bf16), shape((8, 128, 128), bf16)],
+        in_specs=[ANY, ANY, SM, SM, VM],
+        out_specs=[VM, VM],
         scratch_shapes=[
-            pltpu.VMEM((32, 8, 3584), bf16),
-            pltpu.VMEM((8, 16, 384), f32), pltpu.VMEM((8, 16, 384), f32),
-            pltpu.VMEM((8, 16, 384), f32), pltpu.VMEM((8, 16, 384), f32),
+            pltpu.VMEM((32, 8, 1024), bf16), pltpu.VMEM((32, 8, 3584), bf16),
+            gram, gram, gram, gram, gram, gram,
+            pltpu.VMEM((256, 256), f32), pltpu.VMEM((256, 256), f32), pltpu.VMEM((256, 256), f32),
+            pltpu.VMEM((256, 128), f32), pltpu.VMEM((512, 128), f32),
             sem((12,)),
         ],
         compiler_params=pltpu.CompilerParams(
             collective_id=0, has_side_effects=True, vmem_limit_bytes=VMEM_BYTES
         ),
-    )(hidden_stack, model_stack)
-    left, right = pl.pallas_call(
-        core_kernel,
-        out_shape=[shape((4, SERVE_DEV, 128), bf16), shape((8, 128, 128), bf16)],
-        in_specs=[VM, VM, VM, VM, SM, SM, VM],
-        out_specs=[VM, VM],
-        scratch_shapes=[
-            pltpu.VMEM((256, 256), f32), pltpu.VMEM((256, 256), f32), pltpu.VMEM((256, 256), f32),
-            pltpu.VMEM((256, 128), f32), pltpu.VMEM((512, 128), f32),
-        ],
-        compiler_params=pltpu.CompilerParams(vmem_limit_bytes=VMEM_BYTES),
-    )(gm, gh, mbuf, win, tenant_weights, ranks, start_basis)
+    )(hidden_stack, model_stack, tenant_weights, ranks, start_basis)
     lall, rall = pl.pallas_call(
         gather_kernel,
         out_shape=[shape((8, PROJ, SERVE_DEV, 128), bf16), shape((8, PROJ, 8, 128, 128), bf16)],
@@ -520,13 +514,13 @@
     )(left, right)
     return pl.pallas_call(
         tile_kernel,
-        grid=(8, PROJ),
+        grid=(8,),
         out_shape=shape((8, PROJ, SERVE_DEV, 1024), bf16),
         in_specs=[
-            pl.BlockSpec((1, 1, SERVE_DEV, 128), lambda l, p: (l, p, 0, 0)),
-            pl.BlockSpec((1, 1, 8, 128, 128), lambda l, p: (l, p, 0, 0, 0)),
+            pl.BlockSpec((1, PROJ, SERVE_DEV, 128), lambda l: (l, 0, 0, 0)),
+            pl.BlockSpec((1, PROJ, 8, 128, 128), lambda l: (l, 0, 0, 0, 0)),
         ],
-        out_specs=pl.BlockSpec((1, 1, SERVE_DEV, 1024), lambda l, p: (l, p, 0, 0)),
+        out_specs=pl.BlockSpec((1, PROJ, SERVE_DEV, 1024), lambda l: (l, 0, 0, 0)),
     )(lall, rall)
 
 

time: 209 us -> 205 us (0.981)
  Pallas kernels: 202 us -> 199 us
    pallas_call x2 -> x1, Pallas kernels: 86.5 us -> 7.74 us  [shards(): pl.pallas_call(tile_kernel, grid=(8,), out_shape=shape((8, PROJ, SERVE_DE...]
    pallas_call x1, Pallas kernels: 48.6 us -> 126 us  [shards(): pl.pallas_call(core_kernel, out_shape=[shape((4, SERVE_DEV, 128), bf16),...]
where the time goes in v2:
time: 205 us
  Pallas kernels  199 us (97%)
  local copies, waits for them, and re-layouts  5.87 us (3%)
    pallas_call x1, Pallas kernels, shards(): pl.pallas_call(core_kernel, out_shape=[shape((4, SERVE_DEV, 128), bf16),...  126 us
    pallas_call x1, Pallas kernels, shards(): pl.pallas_call(gather_kernel, out_shape=[shape((8, PROJ, SERVE_DEV, 128),...  65.2 us
    pallas_call x1, Pallas kernels, shards(): pl.pallas_call(tile_kernel, grid=(8,), out_shape=shape((8, PROJ, SERVE_DE...  7.74 us
    unnamed x14, local copies, waits for them, and re-layouts  5.87 us

profile of v2, /device:TPU:8, one launch (start us, length us, event | category | flops | bytes accessed | tf_op | source)
XLA Modules:
  0.0 205.0 jit_solution(5153312280625136781)
XLA Ops:
  0.0 0.0 copy-start
  0.0 1.3 copy-done
  1.3 0.0 copy-start.1
  1.3 1.0 copy-done.1
  2.3 0.0 copy-start.3
  2.3 0.9 copy-done.3
  3.2 0.0 copy-start.5
  3.2 0.7 copy-done.5
  3.9 0.0 copy-start.6
  3.9 0.7 copy-done.6
  4.6 126.2 %shard_map.55 = (bf16[4,64,128]{2,1,0:T(8,128)(2,1)S(1)}, bf16[8,128,128]{2,1,0:T(8,128)(2,1)S(1)}) custom-call(bf16[1,3,8,28672]{3,2,1,0:T(8,128)(2,1)S(1)} %copy-done, bf16[1,3,8,8192]{3,2,1,0:T(8,128)(2,1)S(1)} %copy-done.1, f32[8]{0:T(128)S(1)} %copy-done.5, s32[8]{0:T(128)S(1)} %copy-done.6, f32[1,256,128]{2,1,0:T(8,128)S(1)} %copy-done.3), custom_call_target="tpu_custom_call" | custom-call | tf_op jit(solution)/shard_map/pallas_call | solution.py:487
  130.8 0.0 copy-start.2
  130.8 0.7 copy-done.2
  131.5 0.0 copy-start.4
  131.5 0.6 copy-done.4
  132.1 65.2 %shard_map.56 = (bf16[8,3,64,128]{3,2,1,0:T(8,128)(2,1)}, bf16[8,3,8,128,128]{4,3,2,1,0:T(8,128)(2,1)}) custom-call(bf16[4,64,128]{2,1,0:T(8,128)(2,1)} %copy-done.4, bf16[8,128,128]{2,1,0:T(8,128)(2,1)} %copy-done.2), custom_call_target="tpu_custom_call" | custom-call | tf_op jit(solution)/shard_map/pallas_call | solution.py:503
  197.3 7.7 %shard_map.57 = bf16[8,3,64,1024]{3,2,1,0:T(8,128)(2,1)} custom-call(bf16[8,3,64,128]{3,2,1,0:T(8,128)(2,1)} %get-tuple-element.11.left_ref, bf16[8,3,8,128,128]{4,3,2,1,0:T(8,128)(2,1)} %get-tuple-element.12.right_ref), custom_call_target="tpu_custom_call" | custom-call | tf_op jit(solution)/shard_map/pallas_call | solution.py:515
Async XLA Ops:
  0.0 1.3 copy-start
  1.3 1.0 copy-start.1
  2.3 0.9 copy-start.3
  3.2 0.7 copy-start.5
  3.9 0.7 copy-start.6
  130.8 0.7 copy-start.2
  131.5 0.6 copy-start.4

commit v3 on v2

v3 whole, which is shorter than its diff:
```python
import functools
import jax
import jax.numpy as jnp
from jax import lax
from jax.experimental import pallas as pl
from jax.experimental.pallas import tpu as pltpu
from jax.sharding import PartitionSpec as P

ITERS = 3
SERVE_DEV = 64
MOST_RANK = 64
PROJ = 3
SPLIT = 5
HI = lax.Precision.HIGHEST
MESH = pl.DeviceIdType.MESH
VM = pl.BlockSpec(memory_space=pltpu.VMEM)
ANY = pl.BlockSpec(memory_space=pl.ANY)
SM = pl.BlockSpec(memory_space=pltpu.SMEM)
VMEM_BYTES = 48 * 1024 * 1024


def dot_hi(a, b, dims):
    return lax.dot_general(a, b, (dims, ((), ())), precision=HI, preferred_element_type=jnp.float32)


def spread_lane(tile, lane):
    return jnp.broadcast_to(tile[:, lane:lane + 1], (8, 128))


def spread_row(tile, row):
    return jnp.broadcast_to(tile[row:row + 1, :], (8, 128))


def factor(matrix, need_upper, need_inverse):
    sub = lax.broadcasted_iota(jnp.int32, (8, 128), 0)
    lane = lax.broadcasted_iota(jnp.int32, (8, 128), 1)
    rows = [matrix[8 * k:8 * k + 8, :] for k in range(16)]
    inverse = [jnp.where(lane == sub + 8 * k, 1.0, 0.0).astype(jnp.float32) for k in range(16)]
    upper_rows, inverse_rows = [], []
    for k in range(16):
        panel, ipanel = rows[k], inverse[k]
        cols = [spread_lane(panel, 8 * k + c) for c in range(8)]
        raw, iraw, diag = panel, ipanel, panel
        for j in range(8):
            pivot = spread_row(cols[j], j)
            recip = 1.0 / pivot
            scaled = cols[j] * recip
            here = sub == j
            prow = spread_row(panel, j)
            irow = spread_row(ipanel, j)
            raw = jnp.where(here, prow, raw)
            iraw = jnp.where(here, irow, iraw)
            diag = jnp.where(here, pivot, diag)
            panel = jnp.where(here, prow * recip, panel - scaled * prow)
            if need_inverse:
                ipanel = jnp.where(here, irow * recip, ipanel - scaled * irow)
            for c in range(j + 1, 8):
                crow = spread_row(cols[c], j)
                cols[c] = jnp.where(here, crow * recip, cols[c] - scaled * crow)
        root = lax.rsqrt(diag)
        upper_rows.append(raw * root)
        inverse_rows.append(iraw * root)
        prows = [spread_row(panel, c) for c in range(8)]
        irows = [spread_row(ipanel, c) for c in range(8)]
        for i in range(k + 1, 16):
            coef = [spread_lane(rows[i], 8 * k + c) for c in range(8)]
            rows[i] = rows[i] - sum(coef[c] * prows[c] for c in range(8))
            if need_inverse:
                inverse[i] = inverse[i] - sum(coef[c] * irows[c] for c in range(8))
    out = []
    if need_upper:
        rowi = lax.broadcasted_iota(jnp.int32, (128, 128), 0)
        coli = lax.broadcasted_iota(jnp.int32, (128, 128), 1)
        up = jnp.concatenate(upper_rows, axis=0)
        out.append(jnp.where(coli >= rowi, up, 0.0))
    if need_inverse:
        out.append(jnp.concatenate(inverse_rows, axis=0))
    return out


def place():
    layer = lax.axis_index("layer")
    row = lax.axis_index("row")
    return layer, row, row // 4, row % 4


def remote(src, dst, send, recv, layer, row):
    return pltpu.make_async_remote_copy(
        src_ref=src, dst_ref=dst, send_sem=send, recv_sem=recv,
        device_id=(layer, row), device_id_type=MESH,
    )


def wait_bytes(ref, sem):
    pltpu.make_async_copy(ref, ref, sem).wait()


def pack_gram(buf, part):
    ranks = buf.shape[0] * buf.shape[1]
    factors = buf[...].astype(jnp.float32).reshape(ranks, buf.shape[2]).astype(jnp.bfloat16)
    gram = lax.dot_general(
        factors, factors, (((1,), (1,)), ((), ())), preferred_element_type=jnp.float32
    )
    part[:, :, 0:128] = gram[0:128, 0:128].reshape(8, 16, 128)
    part[:, :, 128:384] = gram[128:256, :].reshape(8, 16, 256)


def start_reduce(part, slots, send, recv, layer, z, x):
    def one(k, carry):
        to = (z + k) % 8
        remote(part.at[to], slots.at[z], send, recv, layer, to * 4 + x).start()
        return carry

    lax.fori_loop(1, 8, one, 0)
    slots[pl.ds(z, 1)] = part[pl.ds(z, 1)]


def start_share(slots, out, send, recv, send2, recv2, layer, z, x):
    wait_bytes(slots.at[pl.ds(0, 7)], recv)
    wait_bytes(slots.at[pl.ds(0, 7)], send)
    total = slots[0]
    for k in range(1, 8):
        total = total + slots[k]
    out[pl.ds(z, 1)] = total[None]

    def one(k, carry):
        to = (z + k) % 8
        remote(out.at[z], out.at[z], send2, recv2, layer, to * 4 + x).start()
        return carry

    lax.fori_loop(1, 8, one, 0)


def end_share(out, send2, recv2):
    wait_bytes(out.at[pl.ds(0, 7)], recv2)
    wait_bytes(out.at[pl.ds(0, 7)], send2)


def column_scale(ranks_ref, weights_ref, index):
    total = jnp.zeros(index.shape, jnp.float32)
    begin = 0
    for t in range(8):
        end = begin + ranks_ref[t]
        rank = jnp.full(index.shape, ranks_ref[t].astype(jnp.float32))
        factor_t = weights_ref[t] * jnp.sqrt(MOST_RANK / rank)
        total = jnp.where((index >= begin) & (index < end), factor_t, total)
        begin = end
    return total


def lower_factor(gm_ref, weights_ref, ranks_ref, lower_s, upper_s):
    scale_col = column_scale(ranks_ref, weights_ref, lax.broadcasted_iota(jnp.int32, (256, 1), 0))
    scale_row = column_scale(ranks_ref, weights_ref, lax.broadcasted_iota(jnp.int32, (1, 256), 1))
    packed = gm_ref[...].reshape(128, 384)
    first = packed[:, 0:128] * (scale_col[0:128] * scale_row[:, 0:128])
    cross = packed[:, 128:256] * (scale_col[128:256] * scale_row[:, 0:128])
    last = packed[:, 256:384] * (scale_col[128:256] * scale_row[:, 128:256])
    upper_first, inverse_first = factor(first, True, True)
    low = dot_hi(cross, inverse_first, ((1,), (1,)))
    (upper_last,) = factor(last - dot_hi(low, low, ((1,), (1,))), True, False)
    zero = jnp.zeros((128, 128), jnp.float32)
    upper_s[0:128, 0:128] = upper_first
    upper_s[0:128, 128:256] = low.T
    upper_s[128:256, 0:128] = zero
    upper_s[128:256, 128:256] = upper_last
    lower_s[0:128, 0:128] = upper_first.T
    lower_s[0:128, 128:256] = zero
    lower_s[128:256, 0:128] = low
    lower_s[128:256, 128:256] = upper_last.T


def hidden_map(gh_ref, lower_s, pulled_map):
    packed = gh_ref[...].reshape(128, 384)
    hidden = jnp.concatenate(
        [
            jnp.concatenate([packed[:, 0:128], packed[:, 128:256].T], axis=1),
            packed[:, 128:384],
        ],
        axis=0,
    )
    pulled_map[...] = dot_hi(hidden, lower_s[...], ((1,), (0,)))


def start_sweep(upper_s, pulled_map, both_s):
    pushed = dot_hi(pulled_map[...], both_s[0:256, :], ((1,), (0,)))
    both_s[0:256, :] = dot_hi(upper_s[...], pushed, ((1,), (0,)))
    both_s[256:512, :] = pushed


def one_pass(both_s):
    raised = both_s[0:256, :]
    (inverse,) = factor(dot_hi(raised, raised, ((0,), (0,))), False, True)
    both_s[...] = dot_hi(both_s[...], inverse, ((1,), (1,)))


def window_maps(fbuf, weights_ref, ranks_ref, lower_s, both_s, maps):
    scale_col = column_scale(ranks_ref, weights_ref, lax.broadcasted_iota(jnp.int32, (256, 1), 0))
    lifted = dot_hi(lower_s[...], both_s[0:256, :], ((1,), (0,)))
    pulled = scale_col * both_s[256:512, :]
    for j in range(4):
        window = fbuf[:, :, 896 * j:896 * j + 128].astype(jnp.float32).reshape(256, 128)
        left = dot_hi(window, lifted, ((0,), (0,)))
        left = left[0:SERVE_DEV].astype(jnp.bfloat16).astype(jnp.float32)
        maps[j] = dot_hi(left, pulled, ((1,), (1,))).astype(jnp.bfloat16)


def merge_kernel(f_ref, m_ref, weights_ref, ranks_ref, start_ref, wall, mall, mbuf, fbuf,
                 part_m, part_h, slots_m, slots_h, gm_ref, gh_ref,
                 lower_s, upper_s, pulled_map, both_s, maps, sems,
                 ring_send, ring_recv, side_send, side_recv, wide_send, wide_recv, pass_send, pass_recv,
                 over_send, over_recv):
    layer, row, z, x = place()
    real = x < PROJ
    barrier = pltpu.get_barrier_semaphore()

    def greet(k, carry):
        pl.semaphore_signal(barrier, inc=1, device_id=(layer, (row + k) % 32), device_id_type=MESH)
        return carry

    lax.fori_loop(1, 32, greet, 0)
    for k in range(1, 8):
        pl.semaphore_signal(barrier, inc=1, device_id=((layer + k) % 8, row), device_id_type=MESH)
    pl.semaphore_wait(barrier, 38)

    def row_at(to_z, to_x):
        return (to_z % 8) * 4 + to_x % 4

    mwide, fwide = mbuf.shape[2], fbuf.shape[2]

    def pieces(src_ref, wide, to):
        column = pl.multiple_of((to // 4) * wide, 128)
        return src_ref.at[0, to % 4, :, pl.ds(column, wide)]

    def scatter(src_ref, buf, wide, base, low, high):
        def send(k, carry):
            to = (row + k) % 32

            @pl.when(to % 4 < PROJ)
            def _():
                remote(
                    pieces(src_ref, wide, to), buf.at[row], sems.at[base], sems.at[base + 1], layer, to
                ).start()

            return carry

        lax.fori_loop(low, high, send, 0)

    def keep(src_ref, buf, wide, base):
        pltpu.make_async_copy(pieces(src_ref, wide, row), buf.at[row], sems.at[base + 1]).start()

    def owned(to):
        return m_ref.at[0, :, :, pl.ds(pl.multiple_of(to * 1024, 128), 1024)]

    def shard(p, c, low=0, wide=1024):
        return mall.at[pl.ds(0, SPLIT), :, (c % 8) * 4 + p, :, pl.ds(low, wide)]

    def thick(c, low=0, count=4):
        return mall.at[pl.ds(SPLIT, 8 - SPLIT), :, pl.ds((c % 8) * 4 + low, count)]

    def halves(step, group, up_c, down_c):
        if group:
            return (thick(up_c), thick(down_c)) if step < 3 else (thick(up_c, 0, 2), thick(down_c, 2, 2))
        if step < 3:
            return shard(x, up_c), shard(x, down_c)
        return shard(x, up_c, 0, 512), shard(x, down_c, 512, 512)

    def ring(step, group):
        up, down = halves(step, group, z + 8 - step, z + step)
        return (
            remote(up, up, ring_send.at[group, 0, step], ring_recv.at[group, 0, step], layer, row_at(z + 1, x)),
            remote(down, down, ring_send.at[group, 1, step], ring_recv.at[group, 1, step],
                   layer, row_at(z + 7, x)),
        )

    def ring_start(step, group):
        for copy in ring(step, group):
            copy.start()

    def ring_got(step, group):
        up, down = halves(step, group, z + 7 - step, z + 1 + step)
        wait_bytes(up, ring_recv.at[group, 0, step])
        wait_bytes(down, ring_recv.at[group, 1, step])

    def columns(turn):
        if turn == 0:
            return (z,)
        if turn == 4:
            return (z + 4,)
        return (z + 8 - turn, z + turn)

    def widen(turn):
        for n, c in enumerate(columns(turn)):
            piece = shard(x, c)
            for way in range(2):
                remote(piece, piece, wide_send.at[way, turn, n], wide_recv.at[way, turn, n],
                       layer, row_at(z, x + 1 + 2 * way)).start()

    before, after, far = (x + 3) % 4, (x + 1) % 4, (x + 2) % 4

    def relay(turn):
        for n, c in enumerate(columns(turn)):
            for way, source in enumerate((before, after)):
                wait_bytes(shard(source, c), wide_recv.at[way, turn, n])
                piece = shard(source, c, 512 * way, 512)
                remote(piece, piece, pass_send.at[way, turn, n], pass_recv.at[way, turn, n],
                       layer, row_at(z, x + 1 + 2 * way)).start()

    def relay_end(turn):
        for n, c in enumerate(columns(turn)):
            for way, source in enumerate((before, after)):
                wait_bytes(shard(x, c), wide_send.at[way, turn, n])
                wait_bytes(shard(source, c, 512 * way, 512), pass_send.at[way, turn, n])
                wait_bytes(shard(far, c, 512 * way, 512), pass_recv.at[way, turn, n])

    def narrow(k):
        return mall.at[pl.ds(SPLIT, 8 - SPLIT), :, row_at(z, x + k)]

    def ring_a(step):
        ring_got(step, 0)
        if step < 3:
            ring_start(step + 1, 0)
        widen(step + 1)

    def ring_b(step):
        ring_got(step, 1)
        if step < 3:
            ring_start(step + 1, 1)

    scatter(m_ref, mbuf, mwide, 0, 1, 32)
    for k in range(1, 8):
        to = (layer + k) % 8
        remote(owned(to), mall.at[layer, :, row], sems.at[12], sems.at[13], to, row).start()
    pltpu.make_async_copy(owned(layer), mall.at[layer, :, row], sems.at[13]).start()
    scatter(f_ref, fbuf, fwide, 2, 1, 11)

    @pl.when(real)
    def _():
        keep(m_ref, mbuf, mwide, 0)
        keep(f_ref, fbuf, fwide, 2)
        wait_bytes(mbuf, sems.at[1])
        pack_gram(mbuf, part_m)
        start_reduce(part_m, slots_m, sems.at[4], sems.at[5], layer, z, x)

    scatter(f_ref, fbuf, fwide, 2, 11, 21)

    @pl.when(real)
    def _():
        start_share(slots_m, gm_ref, sems.at[4], sems.at[5], sems.at[6], sems.at[7], layer, z, x)

    scatter(f_ref, fbuf, fwide, 2, 21, 32)
    wait_bytes(mall.at[:, :, row], sems.at[13])
    for k in range(1, 4):
        remote(narrow(0), narrow(0), side_send.at[k - 1], side_recv.at[k - 1], layer, row_at(z, x + k)).start()
    widen(0)

    @pl.when(real)
    def _():
        end_share(gm_ref, sems.at[6], sems.at[7])
        lower_factor(gm_ref, weights_ref, ranks_ref, lower_s, upper_s)
        wait_bytes(fbuf, sems.at[3])
        wait_bytes(mbuf.at[pl.ds(0, 23)], sems.at[0])
        wait_bytes(fbuf.at[pl.ds(0, 23)], sems.at[2])

    @pl.when(jnp.logical_not(real))
    def _():
        wait_bytes(mbuf.at[pl.ds(0, 24)], sems.at[0])
        wait_bytes(fbuf.at[pl.ds(0, 24)], sems.at[2])

    ring_start(0, 0)

    @pl.when(real)
    def _():
        pack_gram(fbuf, part_h)
        start_reduce(part_h, slots_h, sems.at[8], sems.at[9], layer, z, x)
        start_share(slots_h, gh_ref, sems.at[8], sems.at[9], sems.at[10], sems.at[11], layer, z, x)
        end_share(gh_ref, sems.at[10], sems.at[11])
        hidden_map(gh_ref, lower_s, pulled_map)
        both_s[0:256, :] = start_ref[0]

    def stage(i, carry):
        @pl.when(i == 0)
        def _():
            ring_a(0)
            for k in range(1, 4):
                wait_bytes(narrow(4 - k), side_recv.at[k - 1])
            ring_start(0, 1)

        @pl.when(i == 1)
        def _():
            ring_a(1)
            relay(0)

        @pl.when(i == 2)
        def _():
            relay(1)

        @pl.when(i == 3)
        def _():
            ring_b(0)

        @pl.when(i == 4)
        def _():
            ring_a(2)
            relay(2)

        @pl.when(real)
        def _():
            @pl.when(i % 2 == 0)
            def _():
                start_sweep(upper_s, pulled_map, both_s)

            one_pass(both_s)

        return carry

    lax.fori_loop(0, 2 * ITERS, stage, 0)

    @pl.when(real)
    def _():
        window_maps(fbuf, weights_ref, ranks_ref, lower_s, both_s, maps)
        for k in range(1, 4):
            to = (x + k) % 4
            remote(maps.at[to], wall.at[layer, x], sems.at[14], sems.at[15], layer, row_at(z, to)).start()
        pltpu.make_async_copy(maps.at[x], wall.at[layer, x], sems.at[15]).start()

    ring_b(1)
    relay(3)
    ring_a(3)
    other = layer + 1 - 2 * (layer % 2)
    wait_bytes(wall.at[layer], sems.at[15])

    def over(k, index, to):
        return remote(wall.at[index], wall.at[index], over_send.at[k], over_recv.at[k], to, row)

    for k in range(1, 4):
        over(k, layer, (layer + 2 * k) % 8).start()
    over(0, layer, other).start()
    for k in range(1, 4):
        came = (layer + 8 - 2 * k) % 8
        wait_bytes(wall.at[came], over_recv.at[k])
        over(3 + k, came, other).start()
    ring_b(2)
    relay(4)
    ring_b(3)
    for turn in range(5):
        relay_end(turn)
    for step in range(4):
        for group in range(2):
            for copy in ring(step, group):
                copy.wait_send()
    for k in range(1, 4):
        wait_bytes(narrow(0), side_send.at[k - 1])
    wait_bytes(mall.at[pl.ds(0, 7), :, row], sems.at[12])

    @pl.when(real)
    def _():
        wait_bytes(maps.at[pl.ds(0, 3)], sems.at[14])

    wait_bytes(wall.at[other], over_recv.at[0])
    for k in range(1, 4):
        wait_bytes(wall.at[(other + 8 - 2 * k) % 8], over_recv.at[3 + k])
    for k in range(7):
        wait_bytes(wall.at[0], over_send.at[k])


def tile_kernel(maps_ref, model_ref, out_ref):
    for p in range(PROJ):
        model = model_ref[0, p].astype(jnp.float32).reshape(256, 1024).astype(jnp.bfloat16)
        out_ref[0, p] = jnp.dot(
            maps_ref[0, p], model, preferred_element_type=jnp.float32
        ).astype(jnp.bfloat16)


def shards(hidden_stack, model_stack, tenant_weights, ranks, start_basis):
    f32, bf16 = jnp.float32, jnp.bfloat16
    shape = jax.ShapeDtypeStruct
    sem = pltpu.SemaphoreType.DMA
    gram = pltpu.VMEM((8, 16, 384), f32)
    square = pltpu.VMEM((256, 256), f32)
    wall, mall = pl.pallas_call(
        merge_kernel,
        out_shape=[shape((8, PROJ, SERVE_DEV, 256), bf16), shape((8, PROJ, 32, 8, 1024), bf16)],
        in_specs=[ANY, ANY, SM, SM, VM],
        out_specs=[ANY, ANY],
        scratch_shapes=[
            pltpu.VMEM((32, 8, 1024), bf16), pltpu.VMEM((32, 8, 3584), bf16),
            gram, gram, gram, gram, gram, gram,
            square, square, square, pltpu.VMEM((512, 128), f32),
            pltpu.VMEM((4, SERVE_DEV, 256), bf16), sem((16,)),
            sem((2, 2, 4)), sem((2, 2, 4)), sem((3,)), sem((3,)),
            sem((2, 5, 2)), sem((2, 5, 2)), sem((2, 5, 2)), sem((2, 5, 2)),
            sem((7,)), sem((7,)),
        ],
        compiler_params=pltpu.CompilerParams(
            collective_id=0, has_side_effects=True, vmem_limit_bytes=VMEM_BYTES
        ),
    )(hidden_stack, model_stack, tenant_weights, ranks, start_basis)
    return pl.pallas_call(
        tile_kernel,
        grid=(8,),
        out_shape=shape((8, PROJ, SERVE_DEV, 1024), bf16),
        in_specs=[
            pl.BlockSpec((1, PROJ, SERVE_DEV, 256), lambda l: (l, 0, 0, 0)),
            pl.BlockSpec((1, PROJ, 32, 8, 1024), lambda l: (l, 0, 0, 0, 0)),
        ],
        out_specs=pl.BlockSpec((1, PROJ, SERVE_DEV, 1024), lambda l: (l, 0, 0, 0)),
        compiler_params=pltpu.CompilerParams(vmem_limit_bytes=VMEM_BYTES),
    )(wall, mall)


def solution(mesh):
    in_specs = (
        P("layer", None, "row", None),
        P("layer", None, "row", None),
        P(),
        P(),
        P("layer", None, None),
    )
    out_specs = P(None, None, "row", "layer")
    return jax.shard_map(shards, mesh=mesh, in_specs=in_specs, out_specs=out_specs, check_vma=False)
```

time: 205 us -> 166 us (0.81)
  Pallas kernels: 199 us -> 160 us
    pallas_call x2 -> x1, Pallas kernels: 191 us -> 151 us  [shards(): pl.pallas_call(merge_kernel, out_shape=[shape((8, PROJ, SERVE_DEV, 256),...]
    unnamed x14 -> x10, local copies, waits for them, and re-layouts: 5.87 us -> 4.55 us
where the time goes in v3:
time: 166 us; the launch traced here: 165 us
  Pallas kernels  160 us (96%)
  local copies, waits for them, and re-layouts  4.55 us (3%)
    pallas_call x1, Pallas kernels, shards(): pl.pallas_call(merge_kernel, out_shape=[shape((8, PROJ, SERVE_DEV, 256),...  151 us
    pallas_call x1, Pallas kernels, shards(): pl.pallas_call(tile_kernel, grid=(8,), out_shape=shape((8, PROJ, SERVE_DE...  9.43 us
    unnamed x10, local copies, waits for them, and re-layouts  4.55 us

profile of v3, /device:TPU:8, one launch (start us, length us, event | category | flops | bytes accessed | tf_op | source)
XLA Modules:
  0.0 164.8 jit_solution(11060572822982334306)
XLA Ops:
  0.0 0.0 copy-start
  0.0 1.3 copy-done
  1.3 0.0 copy-start.1
  1.3 1.0 copy-done.1
  2.3 0.0 copy-start.2
  2.3 0.9 copy-done.2
  3.2 0.0 copy-start.3
  3.2 0.7 copy-done.3
  3.9 0.0 copy-start.4
  3.9 0.7 copy-done.4
  4.6 150.8 %shard_map.55 = (bf16[8,3,64,256]{3,2,1,0:T(8,128)(2,1)S(1)}, bf16[8,3,32,8,1024]{4,3,2,1,0:T(8,128)(2,1)}) custom-call(bf16[1,3,8,28672]{3,2,1,0:T(8,128)(2,1)S(1)} %copy-done, bf16[1,3,8,8192]{3,2,1,0:T(8,128)(2,1)S(1)} %copy-done.1, f32[8]{0:T(128)S(1)} %copy-done.3, s32[8]{0:T(128)S(1)} %copy-done.4, f32[1,256,128]{2,1,0:T(8,128)S(1)} %copy-done.2), custom_call_target="tpu_custom_call" | custom-call | tf_op jit(solution)/shard_map/pallas_call | solution.py:480
  155.4 9.4 %shard_map.56 = bf16[8,3,64,1024]{3,2,1,0:T(8,128)(2,1)} custom-call(bf16[8,3,64,256]{3,2,1,0:T(8,128)(2,1)S(1)} %get-tuple-element.7.maps_ref, bf16[8,3,32,8,1024]{4,3,2,1,0:T(8,128)(2,1)} %get-tuple-element.8.model_ref), custom_call_target="tpu_custom_call" | custom-call | tf_op jit(solution)/shard_map/pallas_call | solution.py:498
Async XLA Ops:
  0.0 1.3 copy-start
  1.3 1.0 copy-start.1
  2.3 0.9 copy-start.2
  3.2 0.7 copy-start.3
  3.9 0.7 copy-start.4

commit v4 on v3

--- a/solution.py
+++ b/solution.py
@@ -15,8 +15,9 @@
 MESH = pl.DeviceIdType.MESH
 VM = pl.BlockSpec(memory_space=pltpu.VMEM)
 ANY = pl.BlockSpec(memory_space=pl.ANY)
+HBM = pl.BlockSpec(memory_space=pltpu.HBM)
 SM = pl.BlockSpec(memory_space=pltpu.SMEM)
-VMEM_BYTES = 48 * 1024 * 1024
+VMEM_BYTES = 62 * 1024 * 1024
 
 
 def dot_hi(a, b, dims):
@@ -29,52 +30,82 @@
 
 def spread_row(tile, row):
     return jnp.broadcast_to(tile[row:row + 1, :], (8, 128))
+
+
+def total(parts):
+    while len(parts) > 1:
+        parts = [parts[i] + parts[i + 1] for i in range(0, len(parts), 2)]
+    return parts[0]
 
 
 def factor(matrix, need_upper, need_inverse):
     sub = lax.broadcasted_iota(jnp.int32, (8, 128), 0)
     lane = lax.broadcasted_iota(jnp.int32, (8, 128), 1)
+    rowi = lax.broadcasted_iota(jnp.int32, (128, 128), 0)
+    coli = lax.broadcasted_iota(jnp.int32, (128, 128), 1)
+    own = jnp.where(rowi == coli, matrix, 0.0)
+    down = jnp.sum(own, axis=1, keepdims=True)
+    across = jnp.sum(own, axis=0, keepdims=True)
+    unit_down, unit_across = lax.rsqrt(down), lax.rsqrt(across)
+    matrix = matrix * unit_down * unit_across
     rows = [matrix[8 * k:8 * k + 8, :] for k in range(16)]
     inverse = [jnp.where(lane == sub + 8 * k, 1.0, 0.0).astype(jnp.float32) for k in range(16)]
     upper_rows, inverse_rows = [], []
     for k in range(16):
         panel, ipanel = rows[k], inverse[k]
-        cols = [spread_lane(panel, 8 * k + c) for c in range(8)]
+        cols = following if k else [spread_lane(panel, c) for c in range(8)]
+        if k < 15:
+            ahead = [spread_lane(panel, 8 * k + 8 + c) for c in range(8)]
+            raw_next = [spread_lane(rows[k + 1], 8 * k + 8 + c) for c in range(8)]
+            coef_next = [spread_lane(rows[k + 1], 8 * k + c) for c in range(8)]
         raw, iraw, diag = panel, ipanel, panel
-        for j in range(8):
-            pivot = spread_row(cols[j], j)
-            recip = 1.0 / pivot
-            scaled = cols[j] * recip
-            here = sub == j
-            prow = spread_row(panel, j)
-            irow = spread_row(ipanel, j)
-            raw = jnp.where(here, prow, raw)
-            iraw = jnp.where(here, irow, iraw)
-            diag = jnp.where(here, pivot, diag)
-            panel = jnp.where(here, prow * recip, panel - scaled * prow)
+        for j in range(0, 8, 2):
+            first = sub == j
+            second = sub == j + 1
+            a, b, d = spread_row(cols[j], j), spread_row(cols[j], j + 1), spread_row(cols[j + 1], j + 1)
+            recip = 1.0 / (a * d - b * b)
+            aa, ab, bb = d * recip, -b * recip, a * recip
+            one, two = cols[j], cols[j + 1]
+            low = jnp.where(first, -aa, jnp.where(second, -ab, one * aa + two * ab))
+            high = jnp.where(first, -ab, jnp.where(second, -bb, one * ab + two * bb))
+            ratio = b / a
+            diag = jnp.where(first, a, jnp.where(second, d - b * ratio, diag))
+            pair = first | second
+
+            def clear(tile):
+                p, q = spread_row(tile, j), spread_row(tile, j + 1)
+                return p, q, jnp.where(pair, 0.0, tile) - low * p - high * q
+
+            p, q, panel = clear(panel)
+            raw = jnp.where(first, p, jnp.where(second, q - ratio * p, raw))
             if need_inverse:
-                ipanel = jnp.where(here, irow * recip, ipanel - scaled * irow)
-            for c in range(j + 1, 8):
-                crow = spread_row(cols[c], j)
-                cols[c] = jnp.where(here, crow * recip, cols[c] - scaled * crow)
+                p, q, ipanel = clear(ipanel)
+                iraw = jnp.where(first, p, jnp.where(second, q - ratio * p, iraw))
+            for c in range(j + 2, 8):
+                cols[c] = clear(cols[c])[2]
+            if k < 15:
+                ahead = [clear(tile)[2] for tile in ahead]
         root = lax.rsqrt(diag)
         upper_rows.append(raw * root)
         inverse_rows.append(iraw * root)
         prows = [spread_row(panel, c) for c in range(8)]
         irows = [spread_row(ipanel, c) for c in range(8)]
+        if k < 15:
+            following = [
+                raw_next[c] - total([coef_next[j] * spread_row(ahead[c], j) for j in range(8)])
+                for c in range(8)
+            ]
         for i in range(k + 1, 16):
             coef = [spread_lane(rows[i], 8 * k + c) for c in range(8)]
-            rows[i] = rows[i] - sum(coef[c] * prows[c] for c in range(8))
+            rows[i] = rows[i] - total([coef[c] * prows[c] for c in range(8)])
             if need_inverse:
-                inverse[i] = inverse[i] - sum(coef[c] * irows[c] for c in range(8))
+                inverse[i] = inverse[i] - total([coef[c] * irows[c] for c in range(8)])
     out = []
     if need_upper:
-        rowi = lax.broadcasted_iota(jnp.int32, (128, 128), 0)
-        coli = lax.broadcasted_iota(jnp.int32, (128, 128), 1)
-        up = jnp.concatenate(upper_rows, axis=0)
-        out.append(jnp.where(coli >= rowi, up, 0.0))
+        upper = jnp.concatenate(upper_rows, axis=0) * jnp.sqrt(across)
+        out.append(jnp.where(coli >= rowi, upper, 0.0))
     if need_inverse:
-        out.append(jnp.concatenate(inverse_rows, axis=0))
+        out.append(jnp.concatenate(inverse_rows, axis=0) * unit_across)
     return out
 
 
@@ -193,24 +224,48 @@
     both_s[...] = dot_hi(both_s[...], inverse, ((1,), (1,)))
 
 
-def window_maps(fbuf, weights_ref, ranks_ref, lower_s, both_s, maps):
+def halves_of(value):
+    high = value.astype(jnp.bfloat16)
+    return high, (value - high.astype(jnp.float32)).astype(jnp.bfloat16)
+
+
+def dot_halves(a, b, dims):
+    return sum(
+        lax.dot_general(a, half, (dims, ((), ())), preferred_element_type=jnp.float32)
+        for half in halves_of(b)
+    )
+
+
+def keep_windows(fbuf, windows):
+    for j in range(4):
+        window = fbuf[:, :, 896 * j:896 * j + 128].astype(jnp.float32).reshape(256, 128)
+        windows[j] = window.T[0:SERVE_DEV].astype(jnp.bfloat16)
+
+
+def window_maps(windows, weights_ref, ranks_ref, lower_s, both_s, maps):
     scale_col = column_scale(ranks_ref, weights_ref, lax.broadcasted_iota(jnp.int32, (256, 1), 0))
     lifted = dot_hi(lower_s[...], both_s[0:256, :], ((1,), (0,)))
     pulled = scale_col * both_s[256:512, :]
-    for j in range(4):
-        window = fbuf[:, :, 896 * j:896 * j + 128].astype(jnp.float32).reshape(256, 128)
-        left = dot_hi(window, lifted, ((0,), (0,)))
-        left = left[0:SERVE_DEV].astype(jnp.bfloat16).astype(jnp.float32)
-        maps[j] = dot_hi(left, pulled, ((1,), (1,))).astype(jnp.bfloat16)
-
-
-def merge_kernel(f_ref, m_ref, weights_ref, ranks_ref, start_ref, wall, mall, mbuf, fbuf,
+    left = dot_halves(windows[...].reshape(4 * SERVE_DEV, 256), lifted, ((1,), (0,)))
+    product = dot_halves(left.astype(jnp.bfloat16), pulled, ((1,), (1,)))
+    maps[...] = product.astype(jnp.bfloat16).reshape(4, SERVE_DEV, 256)
+
+
+def merge_kernel(f_ref, m_ref, weights_in, ranks_in, start_ref, wall, mall, weights_ref, ranks_ref,
+                 mbuf, fbuf, windows,
                  part_m, part_h, slots_m, slots_h, gm_ref, gh_ref,
                  lower_s, upper_s, pulled_map, both_s, maps, sems,
                  ring_send, ring_recv, side_send, side_recv, wide_send, wide_recv, pass_send, pass_recv,
-                 over_send, over_recv):
+                 over_send, over_recv, map_recv, load_sems):
     layer, row, z, x = place()
     real = x < PROJ
+    loads = [
+        pltpu.make_async_copy(weights_in, weights_ref, load_sems.at[0]),
+        pltpu.make_async_copy(ranks_in, ranks_ref, load_sems.at[1]),
+        pltpu.make_async_copy(start_ref.at[0], both_s.at[pl.ds(0, 256)], load_sems.at[2]),
+    ]
+    for load in loads:
+        load.start()
     barrier = pltpu.get_barrier_semaphore()
 
     def greet(k, carry):
@@ -352,6 +407,9 @@
     for k in range(1, 4):
         remote(narrow(0), narrow(0), side_send.at[k - 1], side_recv.at[k - 1], layer, row_at(z, x + k)).start()
     widen(0)
+    ring_start(0, 0)
+    for load in loads:
+        load.wait()
 
     @pl.when(real)
     def _():
@@ -366,42 +424,54 @@
         wait_bytes(mbuf.at[pl.ds(0, 24)], sems.at[0])
         wait_bytes(fbuf.at[pl.ds(0, 24)], sems.at[2])
 
-    ring_start(0, 0)
-
     @pl.when(real)
     def _():
         pack_gram(fbuf, part_h)
         start_reduce(part_h, slots_h, sems.at[8], sems.at[9], layer, z, x)
+
+    relay(0)
+    ring_a(0)
+
+    @pl.when(real)
+    def _():
+        keep_windows(fbuf, windows)
         start_share(slots_h, gh_ref, sems.at[8], sems.at[9], sems.at[10], sems.at[11], layer, z, x)
+
+    for k in range(1, 4):
+        wait_bytes(narrow(4 - k), side_recv.at[k - 1])
+    ring_start(0, 1)
+
+    @pl.when(real)
+    def _():
         end_share(gh_ref, sems.at[10], sems.at[11])
         hidden_map(gh_ref, lower_s, pulled_map)
-        both_s[0:256, :] = start_ref[0]
 
     def stage(i, carry):
         @pl.when(i == 0)
         def _():
-            ring_a(0)
-            for k in range(1, 4):
-                wait_bytes(narrow(4 - k), side_recv.at[k - 1])
-            ring_start(0, 1)
+            ring_a(1)
 
         @pl.when(i == 1)
         def _():
-            ring_a(1)
-            relay(0)
+            relay(1)
 
         @pl.when(i == 2)
         def _():
-            relay(1)
+            ring_a(2)
+            ring_b(0)
 
         @pl.when(i == 3)
         def _():
-            ring_b(0)
+            relay(2)
 
         @pl.when(i == 4)
         def _():
-            ring_a(2)
-            relay(2)
+            ring_a(3)
+
+        @pl.when(i == 5)
+        def _():
+            ring_b(1)
+            relay(3)
 
         @pl.when(real)
         def _():
@@ -415,32 +485,39 @@
 
     lax.fori_loop(0, 2 * ITERS, stage, 0)
 
-    @pl.when(real)
-    def _():
-        window_maps(fbuf, weights_ref, ranks_ref, lower_s, both_s, maps)
+    other = layer + 1 - 2 * (layer % 2)
+
+    def over(k, index, to):
+        return remote(wall.at[index], wall.at[index], over_send.at[k], over_recv.at[k], to, row)
+
+    def over_part(k, p, to):
+        return remote(wall.at[layer, p], wall.at[layer, p], over_send.at[k], over_recv.at[k], to, row)
+
+    @pl.when(real)
+    def _():
+        window_maps(windows, weights_ref, ranks_ref, lower_s, both_s, maps)
         for k in range(1, 4):
             to = (x + k) % 4
-            remote(maps.at[to], wall.at[layer, x], sems.at[14], sems.at[15], layer, row_at(z, to)).start()
-        pltpu.make_async_copy(maps.at[x], wall.at[layer, x], sems.at[15]).start()
-
-    ring_b(1)
-    relay(3)
-    ring_a(3)
-    other = layer + 1 - 2 * (layer % 2)
-    wait_bytes(wall.at[layer], sems.at[15])
-
-    def over(k, index, to):
-        return remote(wall.at[index], wall.at[index], over_send.at[k], over_recv.at[k], to, row)
-
-    for k in range(1, 4):
-        over(k, layer, (layer + 2 * k) % 8).start()
-    over(0, layer, other).start()
+            remote(maps.at[to], wall.at[layer, x], sems.at[14], map_recv.at[4 - k],
+                   layer, row_at(z, to)).start()
+        pltpu.make_async_copy(maps.at[x], wall.at[layer, x], map_recv.at[0]).start()
+
+    for n in range(4):
+        p = (x + n) % 4
+
+        @pl.when(p < PROJ)
+        def _():
+            wait_bytes(wall.at[layer, p], map_recv.at[n])
+            for k in range(1, 4):
+                over_part(k, p, (layer + 2 * k) % 8).start()
+            over_part(0, p, other).start()
+
+    relay(4)
     for k in range(1, 4):
         came = (layer + 8 - 2 * k) % 8
         wait_bytes(wall.at[came], over_recv.at[k])
         over(3 + k, came, other).start()
     ring_b(2)
-    relay(4)
     ring_b(3)
     for turn in range(5):
         relay_end(turn)
@@ -464,11 +541,12 @@
 
 
 def tile_kernel(maps_ref, model_ref, out_ref):
-    for p in range(PROJ):
-        model = model_ref[0, p].astype(jnp.float32).reshape(256, 1024).astype(jnp.bfloat16)
-        out_ref[0, p] = jnp.dot(
-            maps_ref[0, p], model, preferred_element_type=jnp.float32
-        ).astype(jnp.bfloat16)
+    for i in range(maps_ref.shape[0]):
+        for p in range(PROJ):
+            model = model_ref[i, p].reshape(256, 1024)
+            out_ref[i, p] = jnp.dot(
+                maps_ref[i, p], model, preferred_element_type=jnp.float32
+            ).astype(jnp.bfloat16)
 
 
 def shards(hidden_stack, model_stack, tenant_weights, ranks, start_basis):
@@ -480,16 +558,18 @@
     wall, mall = pl.pallas_call(
         merge_kernel,
         out_shape=[shape((8, PROJ, SERVE_DEV, 256), bf16), shape((8, PROJ, 32, 8, 1024), bf16)],
-        in_specs=[ANY, ANY, SM, SM, VM],
+        in_specs=[HBM] * 5,
         out_specs=[ANY, ANY],
         scratch_shapes=[
+            pltpu.SMEM((8,), f32), pltpu.SMEM((8,), jnp.int32),
             pltpu.VMEM((32, 8, 1024), bf16), pltpu.VMEM((32, 8, 3584), bf16),
+            pltpu.VMEM((4, SERVE_DEV, 256), bf16),
             gram, gram, gram, gram, gram, gram,
             square, square, square, pltpu.VMEM((512, 128), f32),
             pltpu.VMEM((4, SERVE_DEV, 256), bf16), sem((16,)),
             sem((2, 2, 4)), sem((2, 2, 4)), sem((3,)), sem((3,)),
             sem((2, 5, 2)), sem((2, 5, 2)), sem((2, 5, 2)), sem((2, 5, 2)),
-            sem((7,)), sem((7,)),
+            sem((7,)), sem((7,)), sem((4,)), sem((3,)),
         ],
         compiler_params=pltpu.CompilerParams(
             collective_id=0, has_side_effects=True, vmem_limit_bytes=VMEM_BYTES
@@ -497,13 +577,13 @@
     )(hidden_stack, model_stack, tenant_weights, ranks, start_basis)
     return pl.pallas_call(
         tile_kernel,
-        grid=(8,),
+        grid=(2,),
         out_shape=shape((8, PROJ, SERVE_DEV, 1024), bf16),
         in_specs=[
-            pl.BlockSpec((1, PROJ, SERVE_DEV, 256), lambda l: (l, 0, 0, 0)),
-            pl.BlockSpec((1, PROJ, 32, 8, 1024), lambda l: (l, 0, 0, 0, 0)),
+            pl.BlockSpec((4, PROJ, SERVE_DEV, 256), lambda l: (l, 0, 0, 0)),
+            pl.BlockSpec((4, PROJ, 32, 8, 1024), lambda l: (l, 0, 0, 0, 0)),
         ],
-        out_specs=pl.BlockSpec((1, PROJ, SERVE_DEV, 1024), lambda l: (l, 0, 0, 0)),
+        out_specs=pl.BlockSpec((4, PROJ, SERVE_DEV, 1024), lambda l: (l, 0, 0, 0)),
         compiler_params=pltpu.CompilerParams(vmem_limit_bytes=VMEM_BYTES),
     )(wall, mall)
 

time: 166 us -> 149 us (0.90)
  Pallas kernels: 160 us -> 148 us
  local copies, waits for them, and re-layouts: 4.55 us -> 0 us
    pallas_call x1, Pallas kernels: 151 us -> 140 us  [shards(): pl.pallas_call(merge_kernel, out_shape=[shape((8, PROJ, SERVE_DEV, 256),...]
    unnamed x10 -> x0, local copies, waits for them, and re-layouts: 4.55 us -> none
    pallas_call x1, Pallas kernels: 9.43 us -> 7.21 us  [shards(): pl.pallas_call(tile_kernel, grid=(2,), out_shape=shape((8, PROJ, SERVE_DE...]
where the time goes in v4:
time: 149 us; the launch traced here: 148 us
  Pallas kernels  148 us (99%)
    pallas_call x1, Pallas kernels, shards(): pl.pallas_call(merge_kernel, out_shape=[shape((8, PROJ, SERVE_DEV, 256),...  140 us
    pallas_call x1, Pallas kernels, shards(): pl.pallas_call(tile_kernel, grid=(2,), out_shape=shape((8, PROJ, SERVE_DE...  7.21 us

profile of v4, /device:TPU:8, one launch (start us, length us, event | category | flops | bytes accessed | tf_op | source)
XLA Modules:
  0.0 147.7 jit_solution(16765977955155410746)
XLA Ops:
  0.0 140.5 %shard_map.55 = (bf16[8,3,64,256]{3,2,1,0:T(8,128)(2,1)}, bf16[8,3,32,8,1024]{4,3,2,1,0:T(8,128)(2,1)}) custom-call(bf16[1,3,8,28672]{3,2,1,0:T(8,128)(2,1)} %f_ref.1, bf16[1,3,8,8192]{3,2,1,0:T(8,128)(2,1)} %m_ref.1, f32[8]{0:T(128)} %weights_in.1, s32[8]{0:T(128)} %ranks_in.1, f32[1,256,128]{2,1,0:T(8,128)} %start_ref.1), custom_call_target="tpu_custom_call" | custom-call | tf_op jit(solution)/shard_map/pallas_call | solution.py:558
  140.5 7.2 %shard_map.56 = bf16[8,3,64,1024]{3,2,1,0:T(8,128)(2,1)} custom-call(bf16[8,3,64,256]{3,2,1,0:T(8,128)(2,1)} %get-tuple-element.7.maps_ref, bf16[8,3,32,8,1024]{4,3,2,1,0:T(8,128)(2,1)} %get-tuple-element.8.model_ref), custom_call_target="tpu_custom_call" | custom-call | tf_op jit(solution)/shard_map/pallas_call | solution.py:578

commit v5 on v4

--- a/solution.py
+++ b/solution.py
@@ -513,11 +513,11 @@
             over_part(0, p, other).start()
 
     relay(4)
+    ring_b(2)
     for k in range(1, 4):
         came = (layer + 8 - 2 * k) % 8
         wait_bytes(wall.at[came], over_recv.at[k])
         over(3 + k, came, other).start()
-    ring_b(2)
     ring_b(3)
     for turn in range(5):
         relay_end(turn)

time: 149 us -> 147 us (0.987)
  Pallas kernels: 148 us -> 145 us
    pallas_call x1, Pallas kernels: 140 us -> 137 us  [shards(): pl.pallas_call(merge_kernel, out_shape=[shape((8, PROJ, SERVE_DEV, 256),...]
where the time goes in v5:
time: 147 us; the launch traced here: 145 us
  Pallas kernels  145 us (99%)
    pallas_call x1, Pallas kernels, shards(): pl.pallas_call(merge_kernel, out_shape=[shape((8, PROJ, SERVE_DEV, 256),...  137 us
    pallas_call x1, Pallas kernels, shards(): pl.pallas_call(tile_kernel, grid=(2,), out_shape=shape((8, PROJ, SERVE_DE...  7.21 us

profile of v5, /device:TPU:8, one launch (start us, length us, event | category | flops | bytes accessed | tf_op | source)
XLA Modules:
  0.0 144.6 jit_solution(9123123559015931608)
XLA Ops:
  0.0 137.4 %shard_map.55 = (bf16[8,3,64,256]{3,2,1,0:T(8,128)(2,1)}, bf16[8,3,32,8,1024]{4,3,2,1,0:T(8,128)(2,1)}) custom-call(bf16[1,3,8,28672]{3,2,1,0:T(8,128)(2,1)} %f_ref.1, bf16[1,3,8,8192]{3,2,1,0:T(8,128)(2,1)} %m_ref.1, f32[8]{0:T(128)} %weights_in.1, s32[8]{0:T(128)} %ranks_in.1, f32[1,256,128]{2,1,0:T(8,128)} %start_ref.1), custom_call_target="tpu_custom_call" | custom-call | tf_op jit(solution)/shard_map/pallas_call | solution.py:558
  137.4 7.2 %shard_map.56 = bf16[8,3,64,1024]{3,2,1,0:T(8,128)(2,1)} custom-call(bf16[8,3,64,256]{3,2,1,0:T(8,128)(2,1)} %get-tuple-element.7.maps_ref, bf16[8,3,32,8,1024]{4,3,2,1,0:T(8,128)(2,1)} %get-tuple-element.8.model_ref), custom_call_target="tpu_custom_call" | custom-call | tf_op jit(solution)/shard_map/pallas_call | solution.py:578
